TPU v7x, 32 devices: a whole 2x2x4 slice. The times are simulated.
32 devices in a mesh: batch: 8 (over y, x, core), blk: 4 (over z).
Axes of the slice: x: 2, y: 2, z: 4, core: 2. Of those that a mesh axis runs over, the one named last changes fastest.
Arguments:
- hidden_in: bfloat16 [8, 512, 768], P('batch', 'blk'), may hold values from -6 to 6
- w_query: bfloat16 [768, 768], replicated, may hold values from -0.21875 to 0.21875
- b_query: bfloat16 [768], replicated, may hold values from -3 to 3
- w_key: bfloat16 [768, 768], replicated, may hold values from -0.21875 to 0.21875
- w_value: bfloat16 [768, 768], replicated, may hold values from -0.21875 to 0.21875
- b_value: bfloat16 [768], replicated, may hold values from -3 to 3
- w_output: bfloat16 [768, 768], replicated, may hold values from -1.25 to 1.25
- b_output: bfloat16 [768], replicated, may hold values from -3 to 3
- attn_gain: bfloat16 [768], replicated, may hold values from 0.5 to 1.5
- attn_shift: bfloat16 [768], replicated, may hold values from -3 to 3
- w_inner: bfloat16 [768, 3072], replicated, may hold values from -0.21875 to 0.21875
- b_inner: bfloat16 [3072], replicated, may hold values from -3 to 3
- w_outer: bfloat16 [3072, 768], replicated, may hold values from -0.109375 to 0.109375
- b_outer: bfloat16 [768], replicated, may hold values from -3 to 3
- ffn_gain: bfloat16 [768], replicated, may hold values from 0.5 to 1.5
- ffn_shift: bfloat16 [768], replicated, may hold values from -3 to 3
- text_lengths: int32 [8, 4], P('batch'), may hold values from 1 to 64, as said below
- region_lengths: int32 [8, 4], P('batch'), may hold values from 1 to 505
- out_grad: bfloat16 [8, 512, 768], P('batch', 'blk'), may hold values from -6 to 6
Outputs:
- layer_out: bfloat16 [8, 512, 768], P('batch', 'blk')
- grad_in: bfloat16 [8, 512, 768], P('batch', 'blk')
- grad_w_query: float32 [768, 768], P('batch', 'blk')
- grad_b_query: float32 [768], replicated
- grad_w_key: float32 [768, 768], P('batch', 'blk')
- grad_w_value: float32 [768, 768], P('batch', 'blk')
- grad_b_value: float32 [768], replicated
- grad_w_output: float32 [768, 768], P('batch', 'blk')
- grad_b_output: float32 [768], replicated
- grad_attn_gain: float32 [768], replicated
- grad_attn_shift: float32 [768], replicated
- grad_w_inner: float32 [768, 3072], P('batch', 'blk')
- grad_b_inner: float32 [3072], replicated
- grad_w_outer: float32 [3072, 768], P('batch', 'blk')
- grad_b_outer: float32 [768], replicated
- grad_ffn_gain: float32 [768], replicated
- grad_ffn_shift: float32 [768], replicated
Inputs may be any that keep to these rules, and one draw needn't show every extreme that they name: `text_lengths`: in each row the pairs lie end to end from its first position; text and region tokens of all pairs add up to at most 512, and the positions after them are pad.
All inputs are finite; a program needn't handle non-finite values.
Results may differ from a plain program's by a relative error of at most 0.02.
Values may be sent and summed in bfloat16 or wider, within the bound.
No kernel may reach another device: no remote copies, remote signals or barrier semaphores. Data moves between devices by JAX's collectives and lax.ppermute only.
A program may use at most 128 MiB of HBM per device.

v0:
```python
import jax
import jax.numpy as jnp
from jax import lax
from jax.experimental import pallas as pl
from jax.experimental.pallas import tpu as pltpu
from jax.sharding import PartitionSpec as P

HEADS = 12
HEAD_DIM = 64
PAIRS = 4

NORM_EPS = 1e-05
MASKED_SCORE = -1e30
INV_ROOT_TWO = 0.7071067811865476
INV_ROOT_TWO_PI = 0.3989422804014327
MIB = 1024 * 1024

B_OUTER, FFN_GAIN, FFN_SHIFT, ATTN_GAIN, ATTN_SHIFT, B_OUTPUT, B_QUERY, B_VALUE, B_INNER = range(9)

EXTRA = 16

f32 = jnp.float32
bf16 = jnp.bfloat16


def mm(left, right):
    return jnp.dot(left, right, preferred_element_type=f32)


def mm_nt(left, right):
    return lax.dot_general(left, right, (((1,), (1,)), ((), ())), preferred_element_type=f32)


def norm_stats(values_in):
    row_mean = jnp.mean(values_in, axis=-1, keepdims=True)
    centred = values_in - row_mean
    inv_dev = lax.rsqrt(jnp.mean(centred * centred, axis=-1, keepdims=True) + NORM_EPS)
    return centred * inv_dev, inv_dev


def norm_back(scaled, normed, inv_dev):
    centre_term = jnp.mean(scaled, axis=-1, keepdims=True)
    slope_term = jnp.mean(scaled * normed, axis=-1, keepdims=True)
    return inv_dev * (scaled - centre_term - normed * slope_term)


def sum_rows(values):
    return jnp.sum(values, axis=0, keepdims=True)


def as_row(ref):
    return ref[...].astype(f32).reshape(1, -1)


def rows_of(width, count):
    return width // 128 * count


def narrow(ref, first, values):
    count = values.shape[0]
    for k in range(values.shape[1] // 128):
        at = first + k * count
        ref[at : at + count] = values[:, k * 128 : (k + 1) * 128]


def widen(ref, first, count, width):
    return jnp.concatenate(
        [ref[first + k * count : first + (k + 1) * count] for k in range(width // 128)], axis=1
    )


def ahead(me, step, size):
    return lax.rem(me + step, size)


def behind(me, group, size):
    return lax.rem(group - me + size, size)


def prep_kernel(
    text,
    region,
    x_ref,
    grad_ref,
    stacked,
    b_inner,
    w_query,
    w_key,
    w_value,
    w_outer,
    mask,
    vecs,
    x_out,
    grad_out,
    query_out,
    key_out,
    value_out,
    outer_out,
    sems,
):
    me = lax.axis_index("blk")
    row_len = mask.shape[0]
    span = x_ref.shape[0]
    size = row_len // span
    model_width = x_ref.shape[1]
    copies = [
        pltpu.make_async_copy(weight, out, sems.at[k])
        for k, (weight, out) in enumerate(
            (
                (w_query, query_out),
                (w_key, key_out),
                (w_value, value_out),
                (w_outer, outer_out),
            )
        )
    ]
    for copy in copies:
        copy.start()
    x_out[...] = x_ref[...]
    grad_out[...] = grad_ref[...]
    vecs[...] = stacked[...].astype(f32)
    hidden_row = as_row(b_inner)
    for k in range(hidden_row.shape[1] // model_width):
        part = slice(k * model_width, (k + 1) * model_width)
        vecs[B_INNER + k : B_INNER + k + 1] = hidden_row[:, part]

    ends = []
    total = jnp.zeros((1, 1), jnp.int32)
    for k in range(PAIRS):
        total = total + text[:, k : k + 1] + region[:, k : k + 1]
        ends.append(total)

    def segments(dim):
        shape = [1, 1]
        shape[dim] = span
        parts = []
        for s in range(size):
            first = lax.rem(me - s + size, size) * span
            pos = lax.broadcasted_iota(jnp.int32, tuple(shape), dim) + first
            seg = jnp.zeros(tuple(shape), jnp.int32)
            for end in ends:
                seg = seg + (pos >= end).astype(jnp.int32)
            parts.append(seg)
        return jnp.concatenate(parts, axis=dim)

    seg_q = segments(0)
    seg_k = segments(1)
    diagonal = lax.broadcasted_iota(jnp.int32, (row_len, row_len), 0) == lax.broadcasted_iota(
        jnp.int32, (row_len, row_len), 1
    )
    allowed = (seg_q == seg_k) & ((seg_k < PAIRS) | diagonal)
    mask[...] = jnp.where(allowed, 0.0, MASKED_SCORE)
    for copy in copies:
        copy.wait()


def transpose_kernel(w_inner, w_outer, inner_out, inner_t, outer_t, sems):
    copy = pltpu.make_async_copy(w_inner, inner_out, sems.at[0])
    copy.start()
    width, hidden = inner_out.shape
    parts = [slice(k * width, (k + 1) * width) for k in range(hidden // width)]
    for part in parts:
        outer_t[:, part] = w_outer[part].T
    copy.wait()
    for part in parts:
        inner_t[part] = inner_out[:, part].T


def attend(query, key, value, mask_of, tasks, store):
    def scores_of(task):
        part, cols = task
        return mm_nt(query[part, cols], key[:, cols])

    following = scores_of(tasks[0])
    for k, (part, cols) in enumerate(tasks):
        scores = following + mask_of(part)
        if k + 1 < len(tasks):
            following = scores_of(tasks[k + 1])
        weights = jnp.exp(scores - jnp.max(scores, axis=-1, keepdims=True))
        probs = (weights * (1.0 / jnp.sum(weights, axis=-1, keepdims=True))).astype(bf16)
        store(part, cols, probs, mm(probs, value[:, cols]))


def own_attention_kernel(
    x0, x1, x2, x3, w_query, w_key, w_value, vecs, mask, context_ref, x_all
):
    span, width = x0.shape
    for s, ref in enumerate((x0, x1, x2, x3)):
        x_all[s * span : (s + 1) * span] = ref[...]
    query = (mm(x0[...], w_query[...]) + vecs[B_QUERY : B_QUERY + 1]).astype(bf16)
    query = (query * HEAD_DIM ** (-0.5)).astype(bf16)
    key = mm(x_all[...], w_key[...]).astype(bf16)
    value = (mm(x_all[...], w_value[...]) + vecs[B_VALUE : B_VALUE + 1]).astype(bf16)
    rows = slice(0, span)
    tasks = [(rows, slice(h * HEAD_DIM, (h + 1) * HEAD_DIM)) for h in range(width // HEAD_DIM)]
    done = []
    attend(
        query,
        key,
        value,
        lambda part: mask[part],
        tasks,
        lambda part, cols, probs, context: done.append(context),
    )
    context_ref[...] = jnp.concatenate(done, axis=1).astype(bf16)


def head_attention_kernel(
    x0,
    x1,
    x2,
    x3,
    w_query,
    w_key,
    w_value,
    vecs,
    mask,
    order_after,
    probs_ref,
    q_t_ref,
    k_t_ref,
    v_t_ref,
    context_ref,
    x_all,
):
    del order_after
    me = lax.axis_index("blk")
    span = x0.shape[0]
    size = x_all.shape[0] // span
    width = context_ref.shape[1]
    for s, ref in enumerate((x0, x1, x2, x3)):
        x_all[s * span : (s + 1) * span] = ref[...]

    def own_row(k):
        row = vecs[k : k + 1]
        out = jnp.zeros((1, width), f32)
        for g in range(size):
            out = jnp.where(me == g, row[:, g * width : (g + 1) * width], out)
        return out

    def own_cols(ref):
        first = pl.multiple_of((me * width) // 128 * 128, 128)
        window = ref[:, pl.ds(first, 256)]
        return jnp.where((me * width) % 128 == 0, window[:, :width], window[:, 256 - width :])

    query = (mm(x_all[...], own_cols(w_query)) + own_row(B_QUERY)).astype(bf16)
    query = (query * HEAD_DIM ** (-0.5)).astype(bf16)
    key = mm(x_all[...], own_cols(w_key)).astype(bf16)
    value = (mm(x_all[...], own_cols(w_value)) + own_row(B_VALUE)).astype(bf16)
    q_t_ref[...] = query.T
    k_t_ref[...] = key.T
    v_t_ref[...] = value.T
    tasks = [
        (slice(s * span, (s + 1) * span), slice(h * HEAD_DIM, (h + 1) * HEAD_DIM))
        for s in range(size)
        for h in range(width // HEAD_DIM)
    ]

    def store(part, cols, probs, context):
        probs_ref[cols.start // HEAD_DIM, part] = probs
        context_ref[part, cols] = context

    attend(query, key, value, lambda part: mask[part], tasks, store)


def forward_kernel(blocks):
    def body(
        x_ref,
        context_ref,
        vecs,
        grad_ref,
        w_output,
        w_inner,
        w_outer,
        order_after,
        out_ref,
        left_own,
        left_core,
        left_x,
        inner_own,
        inner_core,
        inner_y,
        outer_low_ref,
        slope_ref,
        grad_summed_ref,
        hat_ref,
        inv_ref,
        sums_ref,
        left,
        inner,
    ):
        del order_after
        batch_me = lax.axis_index("batch")
        width, hidden = w_inner.shape
        step = width
        count = hidden // step
        ff_rows = hidden // blocks
        many = left_own.shape[0]
        block = many // (blocks // 4)

        def left_rows(b, first, values):
            at = (b >> 2) * block + first
            left[jnp.bitwise_xor(batch_me & 3, b & 3), at : at + values.shape[0]] = values

        def vec(k):
            return vecs[k : k + 1]

        context = context_ref[...]
        mixed = x_ref[...].astype(f32) + mm(context, w_output[...]) + vec(B_OUTPUT)
        hat, inv = norm_stats(mixed)
        hat_ref[...] = hat
        inv_ref[...] = inv
        attn_norm = hat * vec(ATTN_GAIN) + vec(ATTN_SHIFT)
        inner_in = attn_norm.astype(bf16)
        outer = jnp.zeros(attn_norm.shape, f32)
        cols = [slice(k * step, (k + 1) * step) for k in range(count)]
        following = mm(inner_in, w_inner[:, cols[0]])
        for k in range(count):
            pre = following + vec(B_INNER + k)
            if k + 1 < count:
                following = mm(inner_in, w_inner[:, cols[k + 1]])
            cdf = 0.5 + 0.5 * lax.erf(pre * INV_ROOT_TWO)
            act = (pre * cdf).astype(bf16)
            slope_ref[:, cols[k]] = cdf + pre * (jnp.exp(-0.5 * pre * pre) * INV_ROOT_TWO_PI)
            outer += mm(act, w_outer[cols[k]])
            act_t = act.T
            for j in range(step // ff_rows):
                left_rows(k * step // ff_rows + j, 0, act_t[j * ff_rows : (j + 1) * ff_rows])
        summed = attn_norm + outer + vec(B_OUTER)
        final_hat, final_inv = norm_stats(summed)
        gain = vec(FFN_GAIN)
        upstream = grad_ref[...].astype(f32)
        grad_summed = norm_back(upstream * gain, final_hat, final_inv)
        grad_summed_ref[...] = grad_summed
        outer_low = grad_summed.astype(bf16)
        outer_low_ref[...] = outer_low
        out_ref[...] = (final_hat * gain + vec(FFN_SHIFT)).astype(bf16)
        sums_ref[...] = jnp.zeros(sums_ref.shape, f32)
        sums_ref[B_OUTER : B_OUTER + 1] = sum_rows(outer_low.astype(f32))
        sums_ref[FFN_GAIN : FFN_GAIN + 1] = sum_rows(upstream * final_hat)
        sums_ref[FFN_SHIFT : FFN_SHIFT + 1] = sum_rows(upstream)
        out_rows = width // blocks
        padded = block - ff_rows
        inner_t = inner_in.T
        context_t = context.T

        def block_rows(values, b):
            if padded == out_rows:
                return values[b * out_rows : (b + 1) * out_rows]
            row = lax.broadcasted_iota(jnp.int32, (padded, width), 0)
            col = lax.broadcasted_iota(jnp.int32, (padded, width), 1)
            pick = ((row < out_rows) & (col == row + b * out_rows)).astype(f32).astype(bf16)
            return mm(pick, values).astype(bf16)

        for b in range(blocks):
            left_rows(b, ff_rows, block_rows(context_t, b))
            owner = jnp.bitwise_xor(batch_me & 1, b & 1) + 2 * jnp.bitwise_xor(
                (batch_me >> 2) & 1, (b >> 2) & 1
            )
            at = (((b >> 3) << 1) | ((b >> 1) & 1)) * padded
            inner[owner, at : at + padded] = block_rows(inner_t, b)
        left_own[...] = left[0]
        left_core[...] = left[1]
        left_x[:many] = left[2]
        left_x[many:] = left[3]
        few = inner_own.shape[0]
        inner_own[...] = inner[0]
        inner_core[...] = inner[1]
        inner_y[:few] = inner[2]
        inner_y[few:] = inner[3]

    return body


def backward_kernel(
    outer_low_ref,
    slope_ref,
    grad_summed_ref,
    hat_ref,
    inv_ref,
    left_x,
    inner_y,
    vecs,
    sums_in,
    w_output,
    w_inner_t,
    w_outer_t,
    x_ref,
    y_ref,
    grad_mixed_ref,
    g0,
    g1,
    g2,
    g3,
    groups,
    sums,
):
    hidden, width = w_inner_t.shape
    group_refs = (g0, g1, g2, g3)
    size = len(group_refs)
    me = lax.axis_index("blk")
    step = width
    rows = width // size
    span = outer_low_ref.shape[0]
    count = hidden // step
    parts = [slice(k * step, (k + 1) * step) for k in range(count)]
    sums[...] = sums_in[...]
    outer_low = outer_low_ref[...]
    grad_norm = grad_summed_ref[...]
    many, few = left_x.shape[0], inner_y.shape[0]
    x_ref[:many] = left_x[...]
    y_ref[:few] = inner_y[...]
    following = mm(outer_low, w_outer_t[:, parts[0]])
    for k in range(count):
        pre_low = (following * slope_ref[:, parts[k]]).astype(bf16)
        if k + 1 < count:
            following = mm(outer_low, w_outer_t[:, parts[k + 1]])
        grad_norm += mm(pre_low, w_inner_t[parts[k]])
        y_ref[few + k * step : few + (k + 1) * step] = pre_low.T
        sums[B_INNER + k : B_INNER + k + 1] = sum_rows(pre_low.astype(f32))
    hat = hat_ref[...]
    grad_mixed = norm_back(grad_norm * vecs[ATTN_GAIN : ATTN_GAIN + 1], hat, inv_ref[...])
    grad_mixed_ref[...] = grad_mixed
    mixed_low = grad_mixed.astype(bf16)
    narrow(x_ref, many, outer_low)
    narrow(x_ref, many + rows_of(width, span), mixed_low)
    context_grad_t = mm_nt(w_output[...], mixed_low).astype(bf16)
    for g in range(size):
        groups[behind(me, g, size)] = context_grad_t[g * rows : (g + 1) * rows]
    for s in range(size):
        group_refs[s][...] = groups[s]
    sums[ATTN_GAIN : ATTN_GAIN + 1] = sum_rows(grad_norm * hat)
    sums[ATTN_SHIFT : ATTN_SHIFT + 1] = sum_rows(grad_norm)
    sums[B_OUTPUT : B_OUTPUT + 1] = sum_rows(mixed_low.astype(f32))
    narrow(x_ref, many + 2 * rows_of(width, span), sums[...].astype(bf16))


def pack_kernel(core_rows, own, got, *after_and_out):
    out_ref = after_and_out[-1]
    many = core_rows.shape[0]
    size = own.shape[0] - 2 * many
    out_ref[:many] = core_rows[...]
    out_ref[many : 2 * many] = got[many : 2 * many]
    out_ref[2 * many : 2 * many + size] = own[2 * many :]
    out_ref[2 * many + size :] = got[2 * many :]


def first_products_kernel(block, ff_rows, span):
    def body(left_own, sent, received, packed, send_ref, keep_ref):
        many = left_own.shape[0]
        size = sent.shape[0] - 2 * many
        width = send_ref.shape[1]
        tall = rows_of(width, span)
        own = (lax.axis_index("batch") >> 2) & 1
        lefts = ((left_own, 0), (received, 0), (packed, 0), (packed, many))
        rights = (
            (sent, 2 * many),
            (received, 2 * many),
            (packed, 2 * many),
            (packed, 2 * many + size),
        )
        outer_low = jnp.concatenate([widen(ref, at, span, width) for ref, at in rights], axis=0)
        mixed_low = jnp.concatenate(
            [widen(ref, at + tall, span, width) for ref, at in rights], axis=0
        )
        sums = jnp.zeros((EXTRA, width), f32)
        for ref, at in rights:
            sums += widen(ref, at + 2 * tall, EXTRA, width).astype(f32)
        for ref, side in ((send_ref, 1 - own), (keep_ref, own)):
            count = (ref.shape[0] - EXTRA) // block
            for j in range(count):

                def rows(first, number):
                    start = (2 * j + side) * block + first
                    return jnp.concatenate(
                        [
                            source[pl.ds(pl.multiple_of(start + at, 16), number)]
                            for source, at in lefts
                        ],
                        axis=1,
                    )

                at = j * block
                ref[at : at + ff_rows] = mm(rows(0, ff_rows), outer_low).astype(bf16)
                ref[at + ff_rows : at + block] = mm(
                    rows(ff_rows, block - ff_rows), mixed_low
                ).astype(bf16)
            ref[count * block :] = sums.astype(bf16)

    return body


def inner_products_kernel(block):
    def body(inner_own, sent, received, packed, send_ref, keep_ref):
        few = inner_own.shape[0]
        size = sent.shape[0] - 2 * few
        own = (lax.axis_index("batch") >> 1) & 1
        lefts = ((inner_own, 0), (received, 0), (packed, 0), (packed, few))
        rights = ((sent, 2 * few), (received, 2 * few), (packed, 2 * few), (packed, 2 * few + size))
        pre_t = jnp.concatenate([ref[at : at + size] for ref, at in rights], axis=1)
        many = send_ref.shape[0]
        pieces = []
        for side in (1 - own, own):
            for j in range(many // block):
                start = (2 * j + side) * block
                pieces.append(
                    jnp.concatenate(
                        [
                            source[pl.ds(pl.multiple_of(start + at, 16), block)]
                            for source, at in lefts
                        ],
                        axis=1,
                    )
                )
        total = mm_nt(jnp.concatenate(pieces, axis=0), pre_t).astype(bf16)
        send_ref[...] = total[:many]
        keep_ref[...] = total[many:]

    return body


def halve_kernel(block, bit, parts, extra_rows):
    def body(keep_in, *rest):
        got, (send_ref, keep_ref) = rest[:parts], rest[-2:]
        own = (lax.axis_index("batch") >> bit) & 1
        count = (send_ref.shape[0] - extra_rows) // block

        def total(part):
            added = jnp.concatenate([ref[part] for ref in got], axis=1).astype(f32)
            return (keep_in[part].astype(f32) + added).astype(bf16)

        for ref, side in ((send_ref, 1 - own), (keep_ref, own)):
            for j in range(count):
                start = pl.multiple_of((2 * j + side) * block, 16)
                ref[j * block : (j + 1) * block] = total(pl.ds(start, block))
            if extra_rows:
                last = 2 * count * block
                ref[count * block :] = total(slice(last, last + extra_rows))

    return body


def attention_back_kernel(
    probs_ref,
    q_t_ref,
    k_t_ref,
    v_t_ref,
    context_ref,
    d0,
    d1,
    d2,
    d3,
    e0,
    e1,
    e2,
    e3,
    token_sums,
    score_grad,
    out_t,
):
    slots = (d0, d1, d2, d3)
    outs = (e0, e1, e2, e3)
    size = len(slots)
    width, row_len = q_t_ref.shape
    span = row_len // size
    grad_t = jnp.concatenate([slot[...] for slot in slots], axis=1)
    grad = grad_t.T
    for h in range(width // HEAD_DIM):
        cols = slice(h * HEAD_DIM, (h + 1) * HEAD_DIM)
        for s in range(size):
            part = slice(s * span, (s + 1) * span)
            grad_part = grad[part, cols]
            delta = jnp.sum(
                grad_part.astype(f32) * context_ref[part, cols], axis=-1, keepdims=True
            )
            grad_probs = mm(grad_part, v_t_ref[cols])
            score_grad[part] = (probs_ref[h, part].astype(f32) * (grad_probs - delta)).astype(bf16)
        out_t[cols] = (mm_nt(k_t_ref[cols], score_grad[...]) * HEAD_DIM ** (-0.5)).astype(bf16)
        out_t[width + h * HEAD_DIM : width + (h + 1) * HEAD_DIM] = mm(
            q_t_ref[cols], score_grad[...]
        ).astype(bf16)
        out_t[2 * width + h * HEAD_DIM : 2 * width + (h + 1) * HEAD_DIM] = mm(
            grad_t[cols], probs_ref[h]
        ).astype(bf16)
    for s in range(size):
        outs[s][...] = out_t[:, s * span : (s + 1) * span]
    token_sums[...] = mm_nt(jnp.ones((8, row_len), bf16), out_t[...])


def head_products_kernel(
    x0, x1, x2, x3, e0, e1, e2, e3, token_sums, order_after, send_ref, keep_ref, total
):
    del order_after
    core = lax.axis_index("batch") & 1
    x_t = jnp.concatenate([ref[...].T for ref in (x0, x1, x2, x3)], axis=1)
    heads_t = jnp.concatenate([ref[...] for ref in (e0, e1, e2, e3)], axis=1)
    total[...] = mm_nt(x_t, heads_t)
    blocks = lax.axis_size("batch")
    rows, width = total.shape[0] // blocks, total.shape[1]
    padded = (send_ref.shape[0] - EXTRA) // (blocks // 2)
    for own, refs in ((0, (keep_ref, send_ref)), (1, (send_ref, keep_ref))):

        @pl.when(core == own)
        def _():
            for b in range(blocks):
                at = (b >> 1) * padded
                if padded != rows:
                    refs[b & 1][at : at + padded] = jnp.zeros((padded, width), bf16)
                refs[b & 1][at : at + rows] = total[b * rows : (b + 1) * rows].astype(bf16)

    sums = jnp.concatenate((token_sums[...], jnp.zeros((EXTRA - 8, width), f32)), axis=0)
    for ref in (send_ref, keep_ref):
        ref[(blocks // 2) * padded :] = sums.astype(bf16)


def grad_in_kernel(
    e0, e1, e2, e3, grad_mixed, w_query, w_key, w_value, out_ref, groups, weights, sems
):
    slots = (e0, e1, e2, e3)
    size = len(slots)
    me = lax.axis_index("blk")
    copies = [
        pltpu.make_async_copy(weight, weights.at[k], sems.at[k])
        for k, weight in enumerate((w_query, w_key, w_value))
    ]
    for copy in copies:
        copy.start()
    for s in range(size):
        groups[ahead(me, s, size)] = slots[s][...]
    total = grad_mixed[...]
    own = e0.shape[0] // 3
    for k in range(3):
        rows = [groups[g, k * own : (k + 1) * own] for g in range(size)]
        part = jnp.concatenate(rows, axis=0).T
        copies[k].wait()
        total += mm_nt(part, weights[k])
    out_ref[...] = total.astype(bf16)


def split_inner_kernel(keep, got, own_ref, s1, s2, s3, total):
    outs = (own_ref, s1, s2, s3)
    size = len(outs)
    me = lax.axis_index("blk")
    total[...] = keep[...].astype(f32) + got[...].astype(f32)
    width = total.shape[1] // size
    for s in range(size):
        cols = pl.ds(pl.multiple_of(ahead(me, s, size) * width, 128), width)
        outs[s][...] = total[:, cols].astype(outs[s].dtype)


def join_inner_kernel(own, r1, r2, r3, out_ref):
    rows = slice(0, out_ref.shape[0])
    total = own[rows] + r1[rows].astype(f32) + r2[rows].astype(f32) + r3[rows].astype(f32)
    out_ref[...] = total


def split_columns_kernel(keep, got, late, own_ref, s1, s2, s3, groups):
    outs = (s1, s2, s3)
    size = len(outs) + 1
    me = lax.axis_index("blk")
    total = keep[...].astype(f32) + got[...].astype(f32)
    last = total.shape[0] - EXTRA
    half = last // 2
    width = total.shape[1] // size
    sums = total[last:]
    row = lax.broadcasted_iota(jnp.int32, sums.shape, 0)
    group = lax.broadcasted_iota(jnp.int32, sums.shape, 1) // width
    for k, at in ((B_QUERY, 0), (B_VALUE, 2)):
        own_row = late[0:1, at * width : (at + 1) * width]
        sums = jnp.where(
            (row == k) & (group == me), jnp.concatenate([own_row] * size, axis=1), sums
        )
    extra = jnp.concatenate((sums[:, : 2 * width], sums[:, 2 * width :]), axis=0)
    for g in range(size):
        cols = slice(g * width, (g + 1) * width)
        slot = behind(me, g, size)
        groups[slot, :half] = jnp.concatenate((total[:half, cols], total[half:last, cols]), axis=1)
    own_ref[:half] = groups[0]
    own_ref[half:] = extra
    for s in range(1, size):
        outs[s - 1][:half] = groups[s].astype(bf16)
        outs[s - 1][half:] = extra.astype(bf16)


def join_rows_kernel(own, r1, r2, r3, first_ref, second_ref, *rest):
    sum_refs, (rows,) = rest[:-1], rest[-1:]
    total = own[...] + r1[...].astype(f32) + r2[...].astype(f32) + r3[...].astype(f32)
    half, width = total.shape[0] - 2 * EXTRA, total.shape[1] // 2
    rows[:half] = total[:half, :width]
    rows[half:] = total[:half, width:]
    ff_rows = first_ref.shape[0]
    first_ref[...] = rows[:ff_rows]
    second_ref[...] = rows[ff_rows : ff_rows + second_ref.shape[0]]
    sums = jnp.concatenate((total[half : half + EXTRA], total[half + EXTRA :]), axis=1)
    for k, ref in enumerate(sum_refs[:-1]):
        ref[...] = sums[k]
    model_width = sums.shape[1]
    for k in range(sum_refs[-1].shape[0] // model_width):
        sum_refs[-1][k * model_width : (k + 1) * model_width] = sums[B_INNER + k]


def last_sum_kernel(keep, got, order_after, q_ref, k_ref, v_ref, late_ref):
    del order_after
    total = keep[...].astype(f32) + got[...].astype(f32)
    rows, own = q_ref.shape
    for k, ref in enumerate((q_ref, k_ref, v_ref)):
        ref[...] = total[:rows, k * own : (k + 1) * own]
    last = total.shape[0] - EXTRA
    late_ref[...] = total[last : last + 8]


def run_kernel(body, operands, outs, scratch=(), in_hbm=(), limit=8, fill=0):
    vmem = pl.BlockSpec(memory_space=pltpu.VMEM)
    hbm = pl.BlockSpec(memory_space=pltpu.HBM)
    anywhere = pl.BlockSpec(memory_space=pl.ANY)

    def place(k):
        if k - len(operands) in in_hbm:
            return anywhere
        return hbm if k in in_hbm else vmem

    return pl.pallas_call(
        body,
        out_shape=[jax.ShapeDtypeStruct(shape, dtype) for shape, dtype in outs],
        in_specs=[place(k) for k in range(len(operands))],
        out_specs=[vmem] * len(outs),
        scratch_shapes=list(scratch),
        compiler_params=pltpu.CompilerParams(vmem_limit_bytes=limit * MIB),
        cost_estimate=pl.CostEstimate(
            flops=1 + fill * 10**9, bytes_accessed=1, transcendentals=0
        ),
    )(*operands)


def blk_shift(values, step):
    size = lax.axis_size("blk")
    return lax.ppermute(values, "blk", [(i, (i + step) % size) for i in range(size)])


def batch_swap(values, bits):
    size = lax.axis_size("batch")
    return lax.ppermute(values, "batch", [(i, i ^ bits) for i in range(size)])


def halve(keep, got, block, bit, after=(), extra_rows=EXTRA):
    got = got if isinstance(got, list) else [got]
    count = (keep.shape[0] - extra_rows) // block // 2
    shape = ((count * block + extra_rows, keep.shape[1]), bf16)
    return run_kernel(
        halve_kernel(block, bit, len(got), extra_rows),
        [keep, *got, *after],
        [shape, shape],
        in_hbm=[-1 - k for k in range(len(after))],
    )


def local(
    hidden_in,
    w_query,
    b_query,
    w_key,
    w_value,
    b_value,
    w_output,
    b_output,
    attn_gain,
    attn_shift,
    w_inner,
    b_inner,
    w_outer,
    b_outer,
    ffn_gain,
    ffn_shift,
    text_lengths,
    region_lengths,
    out_grad,
):
    _, span, width = hidden_in.shape
    hidden = w_inner.shape[1]
    size = lax.axis_size("blk")
    blocks = lax.axis_size("batch")
    bits = blocks.bit_length() - 1
    row_len = span * size
    own_heads = HEADS // size
    own_width = own_heads * HEAD_DIM
    steps = range(1, size)
    tokens_f32 = ((span, width), f32)
    tokens_bf16 = ((span, width), bf16)
    row = ((width,), f32)

    flat_in = hidden_in[0]
    x_slots = [blk_shift(flat_in, step) for step in steps]
    stacked = jnp.zeros((EXTRA, width), bf16)
    number = lax.broadcasted_iota(jnp.int32, stacked.shape, 0)
    for k, vector in (
        (B_OUTER, b_outer),
        (FFN_GAIN, ffn_gain),
        (FFN_SHIFT, ffn_shift),
        (ATTN_GAIN, attn_gain),
        (ATTN_SHIFT, attn_shift),
        (B_OUTPUT, b_output),
        (B_QUERY, b_query),
        (B_VALUE, b_value),
    ):
        stacked = jnp.where(number == k, vector[None, :], stacked)
    square = ((width, width), bf16)
    mask, vecs, x_own, grad_own, *attn_weights, outer_copy = run_kernel(
        prep_kernel,
        [
            text_lengths,
            region_lengths,
            flat_in,
            out_grad[0],
            stacked,
            b_inner,
            w_query,
            w_key,
            w_value,
            w_outer,
        ],
        [
            ((row_len, row_len), f32),
            ((EXTRA, width), f32),
            tokens_bf16,
            tokens_bf16,
            square,
            square,
            square,
            ((hidden, width), bf16),
        ],
        [pltpu.SemaphoreType.DMA((4,))],
        in_hbm=(6, 7, 8, 9),
        limit=16,
    )
    inner_copy, *ffn_turned = run_kernel(
        transpose_kernel,
        [w_inner, outer_copy],
        [((width, hidden), bf16), ((hidden, width), bf16), ((width, hidden), bf16)],
        [pltpu.SemaphoreType.DMA((1,))],
        in_hbm=(0,),
        limit=20,
        fill=4,
    )
    ffn_weights = (inner_copy, outer_copy)
    x_slots = [x_own] + x_slots
    context = run_kernel(
        own_attention_kernel,
        x_slots + attn_weights + [vecs, mask],
        [tokens_bf16],
        [pltpu.VMEM((row_len, width), bf16)],
        limit=20,
    )[0]
    ff_rows = hidden // blocks
    rows = -(-(width // blocks) // 16) * 16
    block = ff_rows + rows

    many = blocks // 4 * block
    few = blocks // 4 * rows
    (
        layer_out,
        left_own,
        left_core,
        left_x,
        inner_own,
        inner_core,
        inner_y,
        outer_low,
        slope,
        grad_summed,
        attn_hat,
        attn_inv,
        sums,
    ) = run_kernel(
        forward_kernel(blocks),
        [x_own, context, vecs, grad_own, w_output]
        + [*ffn_weights, ffn_turned[0]],
        [
            tokens_bf16,
            ((many, span), bf16),
            ((many, span), bf16),
            ((2 * many, span), bf16),
            ((few, span), bf16),
            ((few, span), bf16),
            ((2 * few, span), bf16),
            tokens_bf16,
            ((span, hidden), f32),
            tokens_f32,
            tokens_f32,
            ((span, 1), f32),
            ((EXTRA, width), f32),
        ],
        [
            pltpu.VMEM((4, many, span), bf16),
            pltpu.VMEM((4, few, span), bf16),
        ],
        in_hbm=(-1,),
        limit=20,
    )
    tall = 2 * rows_of(width, span) + rows_of(width, EXTRA)
    x_sent, y_sent, grad_mixed, *context_grads = run_kernel(
        backward_kernel,
        [
            outer_low,
            slope,
            grad_summed,
            attn_hat,
            attn_inv,
            left_x,
            inner_y,
            vecs,
            sums,
            w_output,
            *ffn_turned,
        ],
        [((2 * many + tall, span), bf16), ((2 * few + hidden, span), bf16), tokens_f32]
        + [((own_width, span), bf16)] * size,
        [pltpu.VMEM((size, own_width, span), bf16), pltpu.VMEM((EXTRA, width), f32)],
        limit=20,
    )
    x_got = batch_swap(x_sent, 2)
    y_got = batch_swap(y_sent, 4)
    context_grads = context_grads[:1] + [blk_shift(context_grads[step], step) for step in steps]
    heads_shape = ((own_width, row_len), bf16)
    probs, q_t, k_t, v_t, context_own = run_kernel(
        head_attention_kernel,
        x_slots + attn_weights + [vecs, mask, grad_mixed],
        [((own_heads, row_len, row_len), bf16)]
        + [heads_shape] * 3
        + [((row_len, own_width), f32)],
        [pltpu.VMEM((row_len, width), bf16)],
        in_hbm=(-1,),
        limit=16,
        fill=4,
    )
    *head_grads, token_sums = run_kernel(
        attention_back_kernel,
        [probs, q_t, k_t, v_t, context_own] + context_grads,
        [((3 * own_width, span), bf16)] * size + [((8, 3 * own_width), f32)],
        [pltpu.VMEM((row_len, row_len), bf16), pltpu.VMEM((3 * own_width, row_len), bf16)],
    )
    head_slots = head_grads[:1] + [blk_shift(head_grads[step], size - step) for step in steps]
    packed = run_kernel(
        pack_kernel,
        [inner_core, y_sent, y_got, head_slots[1], head_slots[-1]],
        [((2 * (few + hidden), span), bf16)],
        in_hbm=(-1, -2),
        limit=10,
    )[0]
    inner_send, inner_keep = run_kernel(
        inner_products_kernel(rows),
        [inner_own, y_sent, y_got, batch_swap(packed, 1)],
        [((few // 2, hidden), bf16)] * 2,
        limit=14,
    )
    inner_got = batch_swap(inner_send, 2)
    for bit in range(3, bits):
        inner_send, inner_keep = halve(inner_keep, inner_got, rows, bit, extra_rows=0)
        inner_got = batch_swap(inner_send, 1 << bit)
    packed = run_kernel(
        pack_kernel,
        [left_core, x_sent, x_got],
        [((2 * (many + tall), span), bf16)],
    )[0]
    send, keep = run_kernel(
        first_products_kernel(block, ff_rows, span),
        [left_own, x_sent, x_got, batch_swap(packed, 1)],
        [((many // 2 + EXTRA, width), bf16)] * 2,
        limit=14,
    )
    got = batch_swap(send, 4)
    for bit in range(3, bits):
        send, keep = halve(keep, got, block, bit)
        got = batch_swap(send, 1 << bit)
    wide = 3 * own_width
    head_send, head_keep = run_kernel(
        head_products_kernel,
        x_slots + head_grads + [token_sums, send],
        [((blocks // 2 * rows + EXTRA, wide), bf16)] * 2,
        [pltpu.VMEM((width, wide), f32)],
        in_hbm=(-1,),
        limit=10,
    )
    head_got = batch_swap(head_send, 1)
    head_send, head_keep = halve(head_keep, head_got, rows, 1, [inner_got] + head_slots[2:-1])
    head_got = batch_swap(head_send, 2)
    for bit in range(2, bits):
        head_send, head_keep = halve(head_keep, head_got, rows, bit, [got])
        head_got = batch_swap(head_send, 1 << bit)
    inner_part, *inner_sends = run_kernel(
        split_inner_kernel,
        [inner_keep, inner_got],
        [((rows, width), f32)] + [((rows, width), bf16)] * (size - 1),
        [pltpu.VMEM((rows, hidden), f32)],
    )
    inner_parts = [blk_shift(inner_sends[step - 1], step) for step in steps]
    grad_in = run_kernel(
        grad_in_kernel,
        head_slots + [grad_mixed, w_query, w_key, w_value],
        [tokens_bf16],
        [
            pltpu.VMEM((size, 3 * own_width, span), bf16),
            pltpu.VMEM((3, width, width), bf16),
            pltpu.SemaphoreType.DMA((3,)),
        ],
        in_hbm=(5, 6, 7),
        limit=10,
        fill=4,
    )[0]
    out_rows = width // blocks
    own_cols = ((out_rows, own_width), f32)
    *grad_qkv, late = run_kernel(
        last_sum_kernel,
        [head_keep, head_got, inner_parts[1]],
        [own_cols] * 3 + [((8, wide), f32)],
        in_hbm=(-1,),
    )
    message = (block // 2 + 2 * EXTRA, 2 * own_width)
    own_part, *sends = run_kernel(
        split_columns_kernel,
        [keep, got, late],
        [(message, f32)] + [(message, bf16)] * (size - 1),
        [pltpu.VMEM((size, block // 2, 2 * own_width), f32)],
    )
    parts = [blk_shift(sends[step - 1], step) for step in steps]
    grad_w_inner = run_kernel(
        join_inner_kernel, [inner_part] + inner_parts, [((out_rows, width), f32)]
    )[0]
    grad_w_outer, grad_w_output, *sums = run_kernel(
        join_rows_kernel,
        [own_part] + parts,
        [((ff_rows, own_width), f32), own_cols] + [row] * 8 + [((hidden,), f32)],
        [pltpu.VMEM((block, own_width), f32)],
    )
    return (
        layer_out[None],
        grad_in[None],
        grad_qkv[0],
        sums[B_QUERY],
        grad_qkv[1],
        grad_qkv[2],
        sums[B_VALUE],
        grad_w_output,
        sums[B_OUTPUT],
        sums[ATTN_GAIN],
        sums[ATTN_SHIFT],
        grad_w_inner,
        sums[B_INNER],
        grad_w_outer,
        sums[B_OUTER],
        sums[FFN_GAIN],
        sums[FFN_SHIFT],
    )


def solution(mesh):
    rows = P("batch", "blk", None)
    tile = P("batch", "blk")
    return jax.shard_map(
        local,
        mesh=mesh,
        in_specs=(rows,) + (P(),) * 15 + (P("batch", None), P("batch", None), rows),
        out_specs=(
            rows,
            rows,
            tile,
            P(),
            tile,
            tile,
            P(),
            tile,
            P(),
            P(),
            P(),
            tile,
            P(),
            tile,
            P(),
            P(),
            P(),
        ),
        check_vma=False,
    )
```

profile of v0, /device:TPU:0, one launch (start us, length us, event | category | flops | bytes accessed | tf_op | source)
XLA Modules:
  0.0 112.4 jit_solution(10724863308153286557)
XLA Ops:
  0.7 5.1 %collective-permute-start.2 = (bf16[128,768]{1,0:T(8,128)(2,1)}, bf16[128,768]{1,0:T(8,128)(2,1)S(1)}, u32[]{:S(2)}, u32[]{:S(2)}) collective-permute-start(bf16[128,768]{1,0:T(8,128)(2,1)} %bitcast.5), channel_id=1, source_target_pairs={{0,3},{1,0},{2,1},{3,2},{4,7},{5,4},{6,5},{7,6},{8,11},{9,8},{10,9... | collective-permute-start | bytes 589832 | tf_op jit(solution)/shard_map/ppermute | solution.py:737
  5.8 1.0 collective-permute-start
  6.8 0.9 select_select_fusion.stacked
  7.7 2.3 %copy-done.1 = bf16[3072,768]{1,0:T(8,128)(2,1)S(1)} copy-done((bf16[3072,768]{1,0:T(8,128)(2,1)S(1)}, bf16[3072,768]{1,0:T(8,128)(2,1)}, u32[]{:S(2)}) %copy-start.1) | copy-done | bytes 4718616
  10.0 1.3 %copy-done.2 = bf16[768,768]{1,0:T(8,128)(2,1)S(1)} copy-done((bf16[768,768]{1,0:T(8,128)(2,1)S(1)}, bf16[768,768]{1,0:T(8,128)(2,1)}, u32[]{:S(2)}) %copy-start.2) | copy-done | bytes 1179672
  11.3 1.3 %copy-done.4 = bf16[768,768]{1,0:T(8,128)(2,1)S(1)} copy-done((bf16[768,768]{1,0:T(8,128)(2,1)S(1)}, bf16[768,768]{1,0:T(8,128)(2,1)}, u32[]{:S(2)}) %copy-start.4) | copy-done | bytes 1179672
  12.6 1.3 %copy-done.6 = bf16[768,768]{1,0:T(8,128)(2,1)S(1)} copy-done((bf16[768,768]{1,0:T(8,128)(2,1)S(1)}, bf16[768,768]{1,0:T(8,128)(2,1)}, u32[]{:S(2)}) %copy-start.6) | copy-done | bytes 1179672
  13.9 0.9 copy-done.8
  14.8 0.9 copy-done.9
  15.7 0.7 copy-done.10
  17.7 1.4 %shard_map.314 = (f32[512,512]{1,0:T(8,128)S(1)}, f32[16,768]{1,0:T(8,128)S(1)}, bf16[128,768]{1,0:T(8,128)(2,1)S(1)}, bf16[128,768]{1,0:T(8,128)(2,1)S(1)}, bf1...) custom-call(s32[1,4]{1,0:T(1,128)S(1)} %copy-done.11, ...), custom_call_target="tpu_custom_call" | custom-call | flops 1 | bytes 1 | tf_op jit(solution)/shard_map/pallas_call | solution.py:722
  19.1 1.0 copy-done.13
  20.1 3.0 %shard_map.316 = (bf16[768,3072]{1,0:T(8,128)(2,1)S(1)}, bf16[3072,768]{1,0:T(8,128)(2,1)S(1)}, bf16[768,3072]{1,0:T(8,128)(2,1)S(1)}) custom-call(bf16[768,3072]{1,0:T(8,128)(2,1)S(1)} %copy-done.13, bf16[3072,768]{1,0:T(8,128)(2,1)S(1)} %get-tuple-element.98.w_outer), custom_call_target="tpu_custom_call" | custom-call | flops 4000000000 | bytes 1 | tf_op jit(solution)/shard_map/pallas_call | solution.py:722
  23.1 6.1 %shard_map.315.context_ref = bf16[128,768]{1,0:T(8,128)(2,1)S(1)} custom-call(bf16[128,768]{1,0:T(8,128)(2,1)S(1)} %get-tuple-element.91.x0.x_ref, bf16[128,768]{1,0:T(8,128)(2,1)S(1)} %collective-permute-done.x1, bf16[128,768]{1,0:T(8,128)(2,1)S(1)} %collective-permute-done.1.x2, bf16[128,768]{1,0:T(8,128)(2,1)S(1)} %collective-permute-done.2.x3, ...), custom_call_target="tpu_custom_call" | custom-call | flops 1 | bytes 1 | tf_op jit(solution)/shard_map/pallas_call | solution.py:722
  29.2 3.5 %shard_map.317 = (bf16[128,768]{1,0:T(8,128)(2,1)}, bf16[960,128]{1,0:T(8,128)(2,1)S(1)}, bf16[960,128]{1,0:T(8,128)(2,1)S(1)}, bf16[1920,128]{1,0:T(8,128)(2,1)...) custom-call(bf16[128,768]{1,0:T(8,128)(2,1)S(1)} %get-tuple-element., ...), custom_call_target="tpu_custom_call" | custom-call | flops 1 | bytes 1 | tf_op jit(solution)/shard_map/pallas_call | solution.py:722
  32.7 2.2 %shard_map.318 = (bf16[3552,128]{1,0:T(8,128)(2,1)S(1)}, bf16[3456,128]{1,0:T(8,128)(2,1)S(1)}, f32[128,768]{1,0:T(8,128)S(1)}, bf16[192,128]{1,0:T(8,128)(2,1)S...) custom-call(bf16[128,768]{1,0:T(8,128)(2,1)S(1)} %get-tuple-element.102.outer_low_ref,, ...), custom_call_target="tpu_custom_call" | custom-call | flops 1 | bytes 1 | tf_op jit(solution)/shard_map/pallas_call | solution.py:722
  34.9 1.6 %collective-permute-start.12 = (bf16[3456,128]{1,0:T(8,128)(2,1)S(1)}, bf16[3456,128]{1,0:T(8,128)(2,1)S(1)}, u32[]{:S(2)}, u32[]{:S(2)}) collective-permute-start(bf16[3456,128]{1,0:T(8,128)(2,1)S(1)} %get-tuple-element.133.own.sent), channel_id=1, source_target_pairs={{0,16},{4,20},{8,24},{12,28},{16,0},{20,4},{24,8},{28,12},{1,17},{... | collective-permute-start | bytes 2654216 | tf_op jit(solution)/shard_map/ppermute | solution.py:742
  36.5 2.5 %collective-permute-start.3 = (bf16[192,128]{1,0:T(8,128)(2,1)S(1)}, bf16[192,128]{1,0:T(8,128)(2,1)S(1)}, u32[]{:S(2)}, u32[]{:S(2)}) collective-permute-start(bf16[192,128]{1,0:T(8,128)(2,1)S(1)} %get-tuple-element.118), channel_id=1, source_target_pairs={{0,1},{1,2},{2,3},{3,0},{4,5},{5,6},{6,7},{7,4},{8,9},{9,10},{10,1... | collective-permute-start | bytes 147464 | tf_op jit(solution)/shard_map/ppermute | solution.py:737
  39.0 0.9 collective-permute-start.4
  39.9 1.9 %collective-permute-start.5 = (bf16[192,128]{1,0:T(8,128)(2,1)S(1)}, bf16[192,128]{1,0:T(8,128)(2,1)S(1)}, u32[]{:S(2)}, u32[]{:S(2)}) collective-permute-start(bf16[192,128]{1,0:T(8,128)(2,1)S(1)} %get-tuple-element.120), channel_id=1, source_target_pairs={{0,3},{1,0},{2,1},{3,2},{4,7},{5,4},{6,5},{7,6},{8,11},{9,8},{10,9... | collective-permute-start | bytes 147464 | tf_op jit(solution)/shard_map/ppermute | solution.py:737
  41.8 1.5 %collective-permute-start.9 = (bf16[3552,128]{1,0:T(8,128)(2,1)S(1)}, bf16[3552,128]{1,0:T(8,128)(2,1)S(1)}, u32[]{:S(2)}, u32[]{:S(2)}) collective-permute-start(bf16[3552,128]{1,0:T(8,128)(2,1)S(1)} %get-tuple-element.127.own.sent), channel_id=1, source_target_pairs={{0,8},{4,12},{8,0},{12,4},{16,24},{20,28},{24,16},{28,20},{1,9},{5... | collective-permute-start | bytes 2727944 | tf_op jit(solution)/shard_map/ppermute | solution.py:742
  43.3 5.3 %shard_map.319 = (bf16[3,512,512]{2,1,0:T(8,128)(2,1)S(1)}, bf16[192,512]{1,0:T(8,128)(2,1)S(1)}, bf16[192,512]{1,0:T(8,128)(2,1)S(1)}, bf16[192,512]{1,0:T(8,128)(2,1)S(1)}, f32[512,192]{1,0:T(8,128)S(1)}) custom-call(bf16[128,768]{1,0:T(8,128)(2,1)S(1)} %get-tuple-element.91.x0.x_ref, bf16[128,768]{1,0:T(8,128)(2,1)S(1)} %collective-permute-done.x1, ...), custom_call_target="tpu_custom_call" | custom-call | flops 4000000000 | bytes 1 | tf_op jit(solution)/shard_map/pallas_call | solution.py:722
  48.7 2.1 %shard_map.320 = (bf16[576,128]{1,0:T(8,128)(2,1)S(1)}, bf16[576,128]{1,0:T(8,128)(2,1)S(1)}, bf16[576,128]{1,0:T(8,128)(2,1)S(1)}, bf16[576,128]{1,0:T(8,128)(2,1)S(1)}, f32[8,576]{1,0:T(8,128)S(1)}) custom-call(bf16[3,512,512]{2,1,0:T(8,128)(2,1)S(1)} %get-tuple-element.112.probs_ref, bf16[192,512]{1,0:T(8,128)(2,1)S(1)} %get-tuple-element.113.q_t_ref, ...), custom_call_target="tpu_custom_call" | custom-call | flops 1 | bytes 1 | tf_op jit(solution)/shard_map/pallas_call | solution.py:722
  50.8 1.6 %collective-permute-start.6 = (bf16[576,128]{1,0:T(8,128)(2,1)S(1)}, bf16[576,128]{1,0:T(8,128)(2,1)S(1)}, u32[]{:S(2)}, u32[]{:S(2)}) collective-permute-start(bf16[576,128]{1,0:T(8,128)(2,1)S(1)} %get-tuple-element.122.e1), channel_id=1, source_target_pairs={{0,3},{1,0},{2,1},{3,2},{4,7},{5,4},{6,5},{7,6},{8,11},{9,8},{10,9... | collective-permute-start | bytes 442376 | tf_op jit(solution)/shard_map/ppermute | solution.py:737
  52.8 4.5 %collective-permute-done.6.e1.after_and_out_0_ = bf16[576,128]{1,0:T(8,128)(2,1)S(1)} collective-permute-done((bf16[576,128]{1,0:T(8,128)(2,1)S(1)}, bf16[576,128]{1,0:T(8,128)(2,1)S(1)}, u32[]{:S(2)}, u32[]{:S(2)}) %collective-permute-start.6) | collective-permute-done | bytes 147488 | tf_op jit(solution)/shard_map/ppermute | solution.py:737
  57.3 2.0 %collective-permute-done.8.e3.after_and_out_1_ = bf16[576,128]{1,0:T(8,128)(2,1)S(1)} collective-permute-done((bf16[576,128]{1,0:T(8,128)(2,1)S(1)}, bf16[576,128]{1,0:T(8,128)(2,1)S(1)}, u32[]{:S(2)}, u32[]{:S(2)}) %collective-permute-start.8) | collective-permute-done | bytes 147488 | tf_op jit(solution)/shard_map/ppermute | solution.py:737
  59.5 2.5 %collective-permute-done.9.got.received = bf16[3552,128]{1,0:T(8,128)(2,1)S(1)} collective-permute-done((bf16[3552,128]{1,0:T(8,128)(2,1)S(1)}, bf16[3552,128]{1,0:T(8,128)(2,1)S(1)}, u32[]{:S(2)}, u32[]{:S(2)}) %collective-permute-start.9) | collective-permute-done | bytes 909344 | tf_op jit(solution)/shard_map/ppermute | solution.py:742
  62.2 0.8 collective-permute-done.13.packed
  63.0 1.2 %shard_map.326 = (bf16[96,3072]{1,0:T(8,128)(2,1)S(1)}, bf16[96,3072]{1,0:T(8,128)(2,1)S(1)}) custom-call(bf16[192,128]{1,0:T(8,128)(2,1)S(1)} %get-tuple-element.132.inner_own, bf16[3456,128]{1,0:T(8,128)(2,1)S(1)} %get-tuple-element.133.own.sent, bf16[3456,128]{1,0:T(8,128)(2,1)S(1)} %collective-permute-done.12.got.received, ...), custom_call_target="tpu_custom_call" | custom-call | flops 1 | bytes 1 | tf_op jit(solution)/shard_map/pallas_call | solution.py:722
  64.3 0.7 collective-permute-start.14
  65.2 1.0 shard_map.323
  66.9 0.9 shard_map.324
  68.3 9.5 %collective-permute-done.7.e2.rest_2_ = bf16[576,128]{1,0:T(8,128)(2,1)S(1)} collective-permute-done((bf16[576,128]{1,0:T(8,128)(2,1)S(1)}, bf16[576,128]{1,0:T(8,128)(2,1)S(1)}, u32[]{:S(2)}, u32[]{:S(2)}) %collective-permute-start.7) | collective-permute-done | bytes 147488 | tf_op jit(solution)/shard_map/ppermute | solution.py:737
  77.9 1.8 %collective-permute-done.14.rest_1_.got = bf16[96,3072]{1,0:T(8,128)(2,1)S(1)} collective-permute-done((bf16[96,3072]{1,0:T(8,128)(2,1)S(1)}, bf16[96,3072]{1,0:T(8,128)(2,1)S(1)}, u32[]{:S(2)}, u32[]{:S(2)}) %collective-permute-start.14) | collective-permute-done | bytes 589856 | tf_op jit(solution)/shard_map/ppermute | solution.py:742
  79.8 1.1 collective-permute-start.15
  81.5 3.8 %collective-permute-done.16.rest_1_.got = bf16[496,768]{1,0:T(8,128)(2,1)S(1)} collective-permute-done((bf16[496,768]{1,0:T(8,128)(2,1)S(1)}, bf16[496,768]{1,0:T(8,128)(2,1)S(1)}, u32[]{:S(2)}, u32[]{:S(2)}) %collective-permute-start.16) | collective-permute-done | bytes 761888 | tf_op jit(solution)/shard_map/ppermute | solution.py:742
  85.4 2.1 %collective-permute-done.15.rest_0_ = bf16[208,576]{1,0:T(8,128)(2,1)S(1)} collective-permute-done((bf16[208,576]{1,0:T(8,128)(2,1)S(1)}, bf16[208,576]{1,0:T(8,128)(2,1)S(1)}, u32[]{:S(2)}, u32[]{:S(2)}) %collective-permute-start.15) | collective-permute-done | bytes 239648 | tf_op jit(solution)/shard_map/ppermute | solution.py:742
  88.2 3.8 %collective-permute-start.23 = (bf16[96,768]{1,0:T(8,128)(2,1)S(1)}, bf16[96,768]{1,0:T(8,128)(2,1)S(1)}, u32[]{:S(2)}, u32[]{:S(2)}) collective-permute-start(bf16[96,768]{1,0:T(8,128)(2,1)S(1)} %get-tuple-element.159), channel_id=1, source_target_pairs={{0,3},{1,0},{2,1},{3,2},{4,7},{5,4},{6,5},{7,6},{8,11},{9,8},{10,9... | collective-permute-start | bytes 442376 | tf_op jit(solution)/shard_map/ppermute | solution.py:737
  92.0 0.8 collective-permute-done.17.got
  92.8 0.8 shard_map.330
  94.1 1.8 %collective-permute-start.20 = (bf16[272,384]{1,0:T(8,128)(2,1)S(1)}, bf16[272,384]{1,0:T(8,128)(2,1)S(1)}, u32[]{:S(2)}, u32[]{:S(2)}) collective-permute-start(bf16[272,384]{1,0:T(8,128)(2,1)S(1)} %get-tuple-element.147), channel_id=1, source_target_pairs={{0,2},{1,3},{2,0},{3,1},{4,6},{5,7},{6,4},{7,5},{8,10},{9,11},{10,... | collective-permute-start | bytes 626696 | tf_op jit(solution)/shard_map/ppermute | solution.py:737
  95.9 2.0 %collective-permute-start.21 = (bf16[272,384]{1,0:T(8,128)(2,1)S(1)}, bf16[272,384]{1,0:T(8,128)(2,1)S(1)}, u32[]{:S(2)}, u32[]{:S(2)}) collective-permute-start(bf16[272,384]{1,0:T(8,128)(2,1)S(1)} %get-tuple-element.148), channel_id=1, source_target_pairs={{0,3},{1,0},{2,1},{3,2},{4,7},{5,4},{6,5},{7,6},{8,11},{9,8},{10,9... | collective-permute-start | bytes 626696 | tf_op jit(solution)/shard_map/ppermute | solution.py:737
  98.0 3.3 %shard_map.321 = bf16[128,768]{1,0:T(8,128)(2,1)} custom-call(bf16[576,128]{1,0:T(8,128)(2,1)S(1)} %get-tuple-element.121.e0, bf16[576,128]{1,0:T(8,128)(2,1)S(1)} %collective-permute-done.6.e1.after_and_out_0_, bf16[576,128]{1,0:T(8,128)(2,1)S(1)} %collective-permute-done.7.e2.rest_2_, bf16[576,128]{1,0:T(8,128)(2,1)S(1)} %collective-permute-done.8.e3.after_and_out_1_, ...), custom_call_target="tpu_custom_call" | custom-call | flops 4000000000 | bytes 1 | tf_op jit(solution)/shard_map/pallas_call | solution.py:722
  101.3 0.8 shard_map.333
  102.1 2.0 %collective-permute-done.19.r1 = bf16[272,384]{1,0:T(8,128)(2,1)S(1)} collective-permute-done((bf16[272,384]{1,0:T(8,128)(2,1)S(1)}, bf16[272,384]{1,0:T(8,128)(2,1)S(1)}, u32[]{:S(2)}, u32[]{:S(2)}) %collective-permute-start.19) | collective-permute-done | bytes 208928 | tf_op jit(solution)/shard_map/ppermute | solution.py:737
  104.1 6.6 %collective-permute-done.20.r2 = bf16[272,384]{1,0:T(8,128)(2,1)S(1)} collective-permute-done((bf16[272,384]{1,0:T(8,128)(2,1)S(1)}, bf16[272,384]{1,0:T(8,128)(2,1)S(1)}, u32[]{:S(2)}, u32[]{:S(2)}) %collective-permute-start.20) | collective-permute-done | bytes 208928 | tf_op jit(solution)/shard_map/ppermute | solution.py:737
  110.7 0.8 shard_map.332
  111.5 0.9 copy.36
  (54 shorter events, 5.7 us)
Async XLA Ops:
  0.7 22.4 %collective-permute-start.2 = (bf16[128,768]{1,0:T(8,128)(2,1)}, bf16[128,768]{1,0:T(8,128)(2,1)S(1)}, u32[]{:S(2)}, u32[]{:S(2)}) collective-permute-start(bf16[128,768]{1,0:T(8,128)(2,1)} %bitcast.5), channel_id=1, source_target_pairs={{0,3},{1,0},{2,1},{3,2},{4,7},{5,4},{6,5},{7,6},{8,11},{9,8},{10,9... | collective-permute-start | bytes 589832 | tf_op jit(solution)/shard_map/ppermute | solution.py:737
  5.8 17.3 %collective-permute-start.1 = (bf16[128,768]{1,0:T(8,128)(2,1)}, bf16[128,768]{1,0:T(8,128)(2,1)S(1)}, u32[]{:S(2)}, u32[]{:S(2)}) collective-permute-start(bf16[128,768]{1,0:T(8,128)(2,1)} %bitcast.6), channel_id=1, source_target_pairs={{0,2},{1,3},{2,0},{3,1},{4,6},{5,7},{6,4},{7,5},{8,10},{9,11},{10,... | collective-permute-start | bytes 589832 | tf_op jit(solution)/shard_map/ppermute | solution.py:737
  5.8 17.3 %collective-permute-start = (bf16[128,768]{1,0:T(8,128)(2,1)}, bf16[128,768]{1,0:T(8,128)(2,1)S(1)}, u32[]{:S(2)}, u32[]{:S(2)}) collective-permute-start(bf16[128,768]{1,0:T(8,128)(2,1)} %bitcast.7), channel_id=1, source_target_pairs={{0,1},{1,2},{2,3},{3,0},{4,5},{5,6},{6,7},{7,4},{8,9},{9,10},{10,1... | collective-permute-start | bytes 589832 | tf_op jit(solution)/shard_map/ppermute | solution.py:737
  7.7 2.3 %copy-start.1 = (bf16[3072,768]{1,0:T(8,128)(2,1)S(1)}, bf16[3072,768]{1,0:T(8,128)(2,1)}, u32[]{:S(2)}) copy-start(bf16[3072,768]{1,0:T(8,128)(2,1)} %w_outer.1) | copy-start | bytes 14155780
  10.0 1.3 %copy-start.2 = (bf16[768,768]{1,0:T(8,128)(2,1)S(1)}, bf16[768,768]{1,0:T(8,128)(2,1)}, u32[]{:S(2)}) copy-start(bf16[768,768]{1,0:T(8,128)(2,1)} %w_query.3) | copy-start | bytes 3538948
  11.3 1.3 %copy-start.4 = (bf16[768,768]{1,0:T(8,128)(2,1)S(1)}, bf16[768,768]{1,0:T(8,128)(2,1)}, u32[]{:S(2)}) copy-start(bf16[768,768]{1,0:T(8,128)(2,1)} %w_key.3) | copy-start | bytes 3538948
  12.6 1.3 %copy-start.6 = (bf16[768,768]{1,0:T(8,128)(2,1)S(1)}, bf16[768,768]{1,0:T(8,128)(2,1)}, u32[]{:S(2)}) copy-start(bf16[768,768]{1,0:T(8,128)(2,1)} %w_value.3) | copy-start | bytes 3538948
  13.9 0.9 copy-start.8
  14.8 0.9 copy-start.9
  15.7 0.7 copy-start.10
  16.4 0.7 copy-start.11
  17.1 0.7 copy-start.12
  17.7 2.3 %copy-start.13 = (bf16[768,3072]{1,0:T(8,128)(2,1)S(1)}, bf16[768,3072]{1,0:T(8,128)(2,1)}, u32[]{:S(2)}) copy-start(bf16[768,3072]{1,0:T(8,128)(2,1)} %w_inner.1) | copy-start | bytes 14155780
  23.1 6.1 %copy-start = (bf16[768,768]{1,0:T(8,128)(2,1)S(1)}, bf16[768,768]{1,0:T(8,128)(2,1)}, u32[]{:S(2)}) copy-start(bf16[768,768]{1,0:T(8,128)(2,1)} %w_output.3) | copy-start | bytes 3538948
  34.9 24.4 %collective-permute-start.12 = (bf16[3456,128]{1,0:T(8,128)(2,1)S(1)}, bf16[3456,128]{1,0:T(8,128)(2,1)S(1)}, u32[]{:S(2)}, u32[]{:S(2)}) collective-permute-start(bf16[3456,128]{1,0:T(8,128)(2,1)S(1)} %get-tuple-element.133.own.sent), channel_id=1, source_target_pairs={{0,16},{4,20},{8,24},{12,28},{16,0},{20,4},{24,8},{28,12},{1,17},{... | collective-permute-start | bytes 2654216 | tf_op jit(solution)/shard_map/ppermute | solution.py:742
  36.5 12.1 %collective-permute-start.3 = (bf16[192,128]{1,0:T(8,128)(2,1)S(1)}, bf16[192,128]{1,0:T(8,128)(2,1)S(1)}, u32[]{:S(2)}, u32[]{:S(2)}) collective-permute-start(bf16[192,128]{1,0:T(8,128)(2,1)S(1)} %get-tuple-element.118), channel_id=1, source_target_pairs={{0,1},{1,2},{2,3},{3,0},{4,5},{5,6},{6,7},{7,4},{8,9},{9,10},{10,1... | collective-permute-start | bytes 147464 | tf_op jit(solution)/shard_map/ppermute | solution.py:737
  39.0 9.6 %collective-permute-start.4 = (bf16[192,128]{1,0:T(8,128)(2,1)S(1)}, bf16[192,128]{1,0:T(8,128)(2,1)S(1)}, u32[]{:S(2)}, u32[]{:S(2)}) collective-permute-start(bf16[192,128]{1,0:T(8,128)(2,1)S(1)} %get-tuple-element.119), channel_id=1, source_target_pairs={{0,2},{1,3},{2,0},{3,1},{4,6},{5,7},{6,4},{7,5},{8,10},{9,11},{10,... | collective-permute-start | bytes 147464 | tf_op jit(solution)/shard_map/ppermute | solution.py:737
  39.9 8.7 %collective-permute-start.5 = (bf16[192,128]{1,0:T(8,128)(2,1)S(1)}, bf16[192,128]{1,0:T(8,128)(2,1)S(1)}, u32[]{:S(2)}, u32[]{:S(2)}) collective-permute-start(bf16[192,128]{1,0:T(8,128)(2,1)S(1)} %get-tuple-element.120), channel_id=1, source_target_pairs={{0,3},{1,0},{2,1},{3,2},{4,7},{5,4},{6,5},{7,6},{8,11},{9,8},{10,9... | collective-permute-start | bytes 147464 | tf_op jit(solution)/shard_map/ppermute | solution.py:737
  41.8 20.2 %collective-permute-start.9 = (bf16[3552,128]{1,0:T(8,128)(2,1)S(1)}, bf16[3552,128]{1,0:T(8,128)(2,1)S(1)}, u32[]{:S(2)}, u32[]{:S(2)}) collective-permute-start(bf16[3552,128]{1,0:T(8,128)(2,1)S(1)} %get-tuple-element.127.own.sent), channel_id=1, source_target_pairs={{0,8},{4,12},{8,0},{12,4},{16,24},{20,28},{24,16},{28,20},{1,9},{5... | collective-permute-start | bytes 2727944 | tf_op jit(solution)/shard_map/ppermute | solution.py:742
  50.8 6.6 %collective-permute-start.6 = (bf16[576,128]{1,0:T(8,128)(2,1)S(1)}, bf16[576,128]{1,0:T(8,128)(2,1)S(1)}, u32[]{:S(2)}, u32[]{:S(2)}) collective-permute-start(bf16[576,128]{1,0:T(8,128)(2,1)S(1)} %get-tuple-element.122.e1), channel_id=1, source_target_pairs={{0,3},{1,0},{2,1},{3,2},{4,7},{5,4},{6,5},{7,6},{8,11},{9,8},{10,9... | collective-permute-start | bytes 442376 | tf_op jit(solution)/shard_map/ppermute | solution.py:737
  52.4 6.9 %collective-permute-start.8 = (bf16[576,128]{1,0:T(8,128)(2,1)S(1)}, bf16[576,128]{1,0:T(8,128)(2,1)S(1)}, u32[]{:S(2)}, u32[]{:S(2)}) collective-permute-start(bf16[576,128]{1,0:T(8,128)(2,1)S(1)} %get-tuple-element.124.e3), channel_id=1, source_target_pairs={{0,1},{1,2},{2,3},{3,0},{4,5},{5,6},{6,7},{7,4},{8,9},{9,10},{10,1... | collective-permute-start | bytes 442376 | tf_op jit(solution)/shard_map/ppermute | solution.py:737
  59.4 3.6 %collective-permute-start.13 = (bf16[6528,128]{1,0:T(8,128)(2,1)S(1)}, bf16[6528,128]{1,0:T(8,128)(2,1)S(1)}, u32[]{:S(2)}, u32[]{:S(2)}) collective-permute-start(bf16[6528,128]{1,0:T(8,128)(2,1)S(1)} %shard_map.325), channel_id=1, source_target_pairs={{0,4},{4,0},{8,12},{12,8},{16,20},{20,16},{24,28},{28,24},{1,5},{5... | collective-permute-start | bytes 5013512 | tf_op jit(solution)/shard_map/ppermute | solution.py:742
  62.1 3.1 %collective-permute-start.10 = (bf16[5184,128]{1,0:T(8,128)(2,1)S(1)}, bf16[5184,128]{1,0:T(8,128)(2,1)S(1)}, u32[]{:S(2)}, u32[]{:S(2)}) collective-permute-start(bf16[5184,128]{1,0:T(8,128)(2,1)S(1)} %shard_map.322), channel_id=1, source_target_pairs={{0,4},{4,0},{8,12},{12,8},{16,20},{20,16},{24,28},{28,24},{1,5},{5... | collective-permute-start | bytes 3981320 | tf_op jit(solution)/shard_map/ppermute | solution.py:742
  64.3 15.4 %collective-permute-start.14 = (bf16[96,3072]{1,0:T(8,128)(2,1)S(1)}, bf16[96,3072]{1,0:T(8,128)(2,1)S(1)}, u32[]{:S(2)}, u32[]{:S(2)}) collective-permute-start(bf16[96,3072]{1,0:T(8,128)(2,1)S(1)} %get-tuple-element.135), channel_id=1, source_target_pairs={{0,8},{4,12},{8,0},{12,4},{16,24},{20,28},{24,16},{28,20},{1,9},{5... | collective-permute-start | bytes 1769480 | tf_op jit(solution)/shard_map/ppermute | solution.py:742
  66.3 19.1 %collective-permute-start.16 = (bf16[496,768]{1,0:T(8,128)(2,1)S(1)}, bf16[496,768]{1,0:T(8,128)(2,1)S(1)}, u32[]{:S(2)}, u32[]{:S(2)}) collective-permute-start(bf16[496,768]{1,0:T(8,128)(2,1)S(1)} %get-tuple-element.129.order_after), channel_id=1, source_target_pairs={{0,16},{4,20},{8,24},{12,28},{16,0},{20,4},{24,8},{28,12},{1,17},{... | collective-permute-start | bytes 2285576 | tf_op jit(solution)/shard_map/ppermute | solution.py:742
  67.8 10.1 %collective-permute-start.11 = (bf16[400,576]{1,0:T(8,128)(2,1)S(1)}, bf16[400,576]{1,0:T(8,128)(2,1)S(1)}, u32[]{:S(2)}, u32[]{:S(2)}) collective-permute-start(bf16[400,576]{1,0:T(8,128)(2,1)S(1)} %get-tuple-element.131), channel_id=1, source_target_pairs={{0,4},{4,0},{8,12},{12,8},{16,20},{20,16},{24,28},{28,24},{1,5},{5... | collective-permute-start | bytes 1382408 | tf_op jit(solution)/shard_map/ppermute | solution.py:742
  67.8 10.0 %collective-permute-start.7 = (bf16[576,128]{1,0:T(8,128)(2,1)S(1)}, bf16[576,128]{1,0:T(8,128)(2,1)S(1)}, u32[]{:S(2)}, u32[]{:S(2)}) collective-permute-start(bf16[576,128]{1,0:T(8,128)(2,1)S(1)} %get-tuple-element.123.e2), channel_id=1, source_target_pairs={{0,2},{1,3},{2,0},{3,1},{4,6},{5,7},{6,4},{7,5},{8,10},{9,11},{10,... | collective-permute-start | bytes 442376 | tf_op jit(solution)/shard_map/ppermute | solution.py:737
  79.8 7.7 %collective-permute-start.15 = (bf16[208,576]{1,0:T(8,128)(2,1)S(1)}, bf16[208,576]{1,0:T(8,128)(2,1)S(1)}, u32[]{:S(2)}, u32[]{:S(2)}) collective-permute-start(bf16[208,576]{1,0:T(8,128)(2,1)S(1)} %get-tuple-element.137), channel_id=1, source_target_pairs={{0,8},{4,12},{8,0},{12,4},{16,24},{20,28},{24,16},{28,20},{1,9},{5... | collective-permute-start | bytes 718856 | tf_op jit(solution)/shard_map/ppermute | solution.py:742
  80.9 17.1 %copy-start.7 = (bf16[768,768]{1,0:T(8,128)(2,1)S(1)}, bf16[768,768]{1,0:T(8,128)(2,1)}, u32[]{:S(2)}) copy-start(bf16[768,768]{1,0:T(8,128)(2,1)} %w_value.3) | copy-start | bytes 3538948
  81.2 10.8 %collective-permute-start.18 = (bf16[96,768]{1,0:T(8,128)(2,1)S(1)}, bf16[96,768]{1,0:T(8,128)(2,1)S(1)}, u32[]{:S(2)}, u32[]{:S(2)}) collective-permute-start(bf16[96,768]{1,0:T(8,128)(2,1)S(1)} %get-tuple-element.141), channel_id=1, source_target_pairs={{0,2},{1,3},{2,0},{3,1},{4,6},{5,7},{6,4},{7,5},{8,10},{9,11},{10,... | collective-permute-start | bytes 442376 | tf_op jit(solution)/shard_map/ppermute | solution.py:737
  87.5 10.5 %copy-start.3 = (bf16[768,768]{1,0:T(8,128)(2,1)S(1)}, bf16[768,768]{1,0:T(8,128)(2,1)}, u32[]{:S(2)}) copy-start(bf16[768,768]{1,0:T(8,128)(2,1)} %w_query.3) | copy-start | bytes 3538948
  87.5 10.5 %copy-start.5 = (bf16[768,768]{1,0:T(8,128)(2,1)S(1)}, bf16[768,768]{1,0:T(8,128)(2,1)}, u32[]{:S(2)}) copy-start(bf16[768,768]{1,0:T(8,128)(2,1)} %w_key.3) | copy-start | bytes 3538948
  87.6 5.2 %collective-permute-start.17 = (bf16[112,576]{1,0:T(8,128)(2,1)S(1)}, bf16[112,576]{1,0:T(8,128)(2,1)S(1)}, u32[]{:S(2)}, u32[]{:S(2)}) collective-permute-start(bf16[112,576]{1,0:T(8,128)(2,1)S(1)} %get-tuple-element.139), channel_id=1, source_target_pairs={{0,16},{4,20},{8,24},{12,28},{16,0},{20,4},{24,8},{28,12},{1,17},{... | collective-permute-start | bytes 387080 | tf_op jit(solution)/shard_map/ppermute | solution.py:742
  88.2 13.1 %collective-permute-start.22 = (bf16[96,768]{1,0:T(8,128)(2,1)S(1)}, bf16[96,768]{1,0:T(8,128)(2,1)S(1)}, u32[]{:S(2)}, u32[]{:S(2)}) collective-permute-start(bf16[96,768]{1,0:T(8,128)(2,1)S(1)} %get-tuple-element.158), channel_id=1, source_target_pairs={{0,1},{1,2},{2,3},{3,0},{4,5},{5,6},{6,7},{7,4},{8,9},{9,10},{10,1... | collective-permute-start | bytes 442376 | tf_op jit(solution)/shard_map/ppermute | solution.py:737
  88.2 13.1 %collective-permute-start.23 = (bf16[96,768]{1,0:T(8,128)(2,1)S(1)}, bf16[96,768]{1,0:T(8,128)(2,1)S(1)}, u32[]{:S(2)}, u32[]{:S(2)}) collective-permute-start(bf16[96,768]{1,0:T(8,128)(2,1)S(1)} %get-tuple-element.159), channel_id=1, source_target_pairs={{0,3},{1,0},{2,1},{3,2},{4,7},{5,4},{6,5},{7,6},{8,11},{9,8},{10,9... | collective-permute-start | bytes 442376 | tf_op jit(solution)/shard_map/ppermute | solution.py:737
  94.1 10.0 %collective-permute-start.19 = (bf16[272,384]{1,0:T(8,128)(2,1)S(1)}, bf16[272,384]{1,0:T(8,128)(2,1)S(1)}, u32[]{:S(2)}, u32[]{:S(2)}) collective-permute-start(bf16[272,384]{1,0:T(8,128)(2,1)S(1)} %get-tuple-element.146), channel_id=1, source_target_pairs={{0,1},{1,2},{2,3},{3,0},{4,5},{5,6},{6,7},{7,4},{8,9},{9,10},{10,1... | collective-permute-start | bytes 626696 | tf_op jit(solution)/shard_map/ppermute | solution.py:737
  94.1 16.5 %collective-permute-start.20 = (bf16[272,384]{1,0:T(8,128)(2,1)S(1)}, bf16[272,384]{1,0:T(8,128)(2,1)S(1)}, u32[]{:S(2)}, u32[]{:S(2)}) collective-permute-start(bf16[272,384]{1,0:T(8,128)(2,1)S(1)} %get-tuple-element.147), channel_id=1, source_target_pairs={{0,2},{1,3},{2,0},{3,1},{4,6},{5,7},{6,4},{7,5},{8,10},{9,11},{10,... | collective-permute-start | bytes 626696 | tf_op jit(solution)/shard_map/ppermute | solution.py:737
  95.9 14.7 %collective-permute-start.21 = (bf16[272,384]{1,0:T(8,128)(2,1)S(1)}, bf16[272,384]{1,0:T(8,128)(2,1)S(1)}, u32[]{:S(2)}, u32[]{:S(2)}) collective-permute-start(bf16[272,384]{1,0:T(8,128)(2,1)S(1)} %get-tuple-element.148), channel_id=1, source_target_pairs={{0,3},{1,0},{2,1},{3,2},{4,7},{5,4},{6,5},{7,6},{8,11},{9,8},{10,9... | collective-permute-start | bytes 626696 | tf_op jit(solution)/shard_map/ppermute | solution.py:737
where the time goes:
time: 114 us; the launch traced here: 112 us
  waiting for transfers between devices  36.9 us (32%)
  Pallas kernels  33.6 us (29%)
  starting transfers between devices  28.2 us (25%)
  local copies, waits for them, and re-layouts  11.8 us (10%)
    pallas_call x20, Pallas kernels, run_kernel(): pl.pallas_call(body, out_shape=[jax.ShapeDtypeStruct(shape, dtype) for sh...  33.6 us
    ppermute x15, waiting for transfers between devices, blk_shift(): lax.ppermute(values, 'blk', [(i, (i + step) % size) for i in range(size)])  24.6 us
    ppermute x15, starting transfers between devices, blk_shift(): lax.ppermute(values, 'blk', [(i, (i + step) % size) for i in range(size)])  22 us
    ppermute x9, waiting for transfers between devices, batch_swap(): return lax.ppermute(values, 'batch', [(i, i ^ bits) for i in range(size)])  12.2 us
    unnamed x29, local copies, waits for them, and re-layouts  11.8 us
    ppermute x9, starting transfers between devices, batch_swap(): return lax.ppermute(values, 'batch', [(i, i ^ bits) for i in range(size)])  6.21 us
  transfers between devices with their start and end apart: 24, of which 12 were waited for; matrix products, arithmetic and copies ran while one was open for 1% of the time, Pallas kernels for 19%

commit v1 on v0

--- a/solution.py
+++ b/solution.py
@@ -930,7 +930,6 @@
         [pltpu.VMEM((row_len, width), bf16)],
         in_hbm=(-1,),
         limit=16,
-        fill=4,
     )
     *head_grads, token_sums = run_kernel(
         attention_back_kernel,
@@ -941,9 +940,9 @@
     head_slots = head_grads[:1] + [blk_shift(head_grads[step], size - step) for step in steps]
     packed = run_kernel(
         pack_kernel,
-        [inner_core, y_sent, y_got, head_slots[1], head_slots[-1]],
+        [inner_core, y_sent, y_got, head_slots[1]],
         [((2 * (few + hidden), span), bf16)],
-        in_hbm=(-1, -2),
+        in_hbm=(-1,),
         limit=10,
     )[0]
     inner_send, inner_keep = run_kernel(
@@ -981,7 +980,7 @@
         limit=10,
     )
     head_got = batch_swap(head_send, 1)
-    head_send, head_keep = halve(head_keep, head_got, rows, 1, [inner_got] + head_slots[2:-1])
+    head_send, head_keep = halve(head_keep, head_got, rows, 1, [inner_got] + head_slots[2:])
     head_got = batch_swap(head_send, 2)
     for bit in range(2, bits):
         head_send, head_keep = halve(head_keep, head_got, rows, bit, [got])

time: 114 us -> 115 us (level)
  starting transfers between devices: 28.2 us -> 35.3 us
  waiting for transfers between devices: 36.9 us -> 30.9 us
    ppermute x15, starting transfers between devices: 22 us -> 28 us  [blk_shift(): lax.ppermute(values, 'blk', [(i, (i + step) % size) for i in range(size)])]
    ppermute x9, waiting for transfers between devices: 12.2 us -> 8.89 us  [batch_swap(): return lax.ppermute(values, 'batch', [(i, i ^ bits) for i in range(size)])]
    ppermute x15, waiting for transfers between devices: 24.6 us -> 22 us  [blk_shift(): lax.ppermute(values, 'blk', [(i, (i + step) % size) for i in range(size)])]
  transfers between devices with their start and end apart: 24 -> 24, of which waited for: 12 -> 8; matrix products, arithmetic and copies ran while one was open for 1% -> 1% of each run, Pallas kernels for 19% -> 18%
where the time goes in v1:
time: 115 us; the launch traced here: 113 us
  starting transfers between devices  35.3 us (31%)
  Pallas kernels  33.7 us (29%)
  waiting for transfers between devices  30.9 us (27%)
  local copies, waits for them, and re-layouts  11.9 us (10%)
    pallas_call x20, Pallas kernels, run_kernel(): pl.pallas_call(body, out_shape=[jax.ShapeDtypeStruct(shape, dtype) for sh...  33.7 us
    ppermute x15, starting transfers between devices, blk_shift(): lax.ppermute(values, 'blk', [(i, (i + step) % size) for i in range(size)])  28 us
    ppermute x15, waiting for transfers between devices, blk_shift(): lax.ppermute(values, 'blk', [(i, (i + step) % size) for i in range(size)])  22 us
    unnamed x29, local copies, waits for them, and re-layouts  11.9 us
    ppermute x9, waiting for transfers between devices, batch_swap(): return lax.ppermute(values, 'batch', [(i, i ^ bits) for i in range(size)])  8.89 us
    ppermute x9, starting transfers between devices, batch_swap(): return lax.ppermute(values, 'batch', [(i, i ^ bits) for i in range(size)])  7.28 us
  transfers between devices with their start and end apart: 24, of which 8 were waited for; matrix products, arithmetic and copies ran while one was open for 1% of the time, Pallas kernels for 18%

profile of v1, /device:TPU:0, one launch (start us, length us, event | category | flops | bytes accessed | tf_op | source)
XLA Modules:
  0.0 113.5 jit_solution(1046680475682128765)
XLA Ops:
  0.7 5.1 %collective-permute-start.2 = (bf16[128,768]{1,0:T(8,128)(2,1)}, bf16[128,768]{1,0:T(8,128)(2,1)S(1)}, u32[]{:S(2)}, u32[]{:S(2)}) collective-permute-start(bf16[128,768]{1,0:T(8,128)(2,1)} %bitcast.5), channel_id=1, source_target_pairs={{0,3},{1,0},{2,1},{3,2},{4,7},{5,4},{6,5},{7,6},{8,11},{9,8},{10,9... | collective-permute-start | bytes 589832 | tf_op jit(solution)/shard_map/ppermute | solution.py:737
  5.8 1.0 collective-permute-start
  6.8 0.9 select_select_fusion.stacked
  7.7 2.3 %copy-done.1 = bf16[3072,768]{1,0:T(8,128)(2,1)S(1)} copy-done((bf16[3072,768]{1,0:T(8,128)(2,1)S(1)}, bf16[3072,768]{1,0:T(8,128)(2,1)}, u32[]{:S(2)}) %copy-start.1) | copy-done | bytes 4718616
  10.0 1.3 %copy-done.2 = bf16[768,768]{1,0:T(8,128)(2,1)S(1)} copy-done((bf16[768,768]{1,0:T(8,128)(2,1)S(1)}, bf16[768,768]{1,0:T(8,128)(2,1)}, u32[]{:S(2)}) %copy-start.2) | copy-done | bytes 1179672
  11.3 1.3 %copy-done.4 = bf16[768,768]{1,0:T(8,128)(2,1)S(1)} copy-done((bf16[768,768]{1,0:T(8,128)(2,1)S(1)}, bf16[768,768]{1,0:T(8,128)(2,1)}, u32[]{:S(2)}) %copy-start.4) | copy-done | bytes 1179672
  12.6 1.3 %copy-done.6 = bf16[768,768]{1,0:T(8,128)(2,1)S(1)} copy-done((bf16[768,768]{1,0:T(8,128)(2,1)S(1)}, bf16[768,768]{1,0:T(8,128)(2,1)}, u32[]{:S(2)}) %copy-start.6) | copy-done | bytes 1179672
  13.9 0.9 copy-done.8
  14.8 0.9 copy-done.9
  15.7 0.7 copy-done.10
  17.7 1.4 %shard_map.314 = (f32[512,512]{1,0:T(8,128)S(1)}, f32[16,768]{1,0:T(8,128)S(1)}, bf16[128,768]{1,0:T(8,128)(2,1)S(1)}, bf16[128,768]{1,0:T(8,128)(2,1)S(1)}, bf1...) custom-call(s32[1,4]{1,0:T(1,128)S(1)} %copy-done.11, ...), custom_call_target="tpu_custom_call" | custom-call | flops 1 | bytes 1 | tf_op jit(solution)/shard_map/pallas_call | solution.py:722
  19.1 1.0 copy-done.13
  20.1 3.0 %shard_map.316 = (bf16[768,3072]{1,0:T(8,128)(2,1)S(1)}, bf16[3072,768]{1,0:T(8,128)(2,1)S(1)}, bf16[768,3072]{1,0:T(8,128)(2,1)S(1)}) custom-call(bf16[768,3072]{1,0:T(8,128)(2,1)S(1)} %copy-done.13, bf16[3072,768]{1,0:T(8,128)(2,1)S(1)} %get-tuple-element.98.w_outer), custom_call_target="tpu_custom_call" | custom-call | flops 4000000000 | bytes 1 | tf_op jit(solution)/shard_map/pallas_call | solution.py:722
  23.1 6.1 %shard_map.315.context_ref = bf16[128,768]{1,0:T(8,128)(2,1)S(1)} custom-call(bf16[128,768]{1,0:T(8,128)(2,1)S(1)} %get-tuple-element.91.x0.x_ref, bf16[128,768]{1,0:T(8,128)(2,1)S(1)} %collective-permute-done.x1, bf16[128,768]{1,0:T(8,128)(2,1)S(1)} %collective-permute-done.1.x2, bf16[128,768]{1,0:T(8,128)(2,1)S(1)} %collective-permute-done.2.x3, ...), custom_call_target="tpu_custom_call" | custom-call | flops 1 | bytes 1 | tf_op jit(solution)/shard_map/pallas_call | solution.py:722
  29.2 3.5 %shard_map.317 = (bf16[128,768]{1,0:T(8,128)(2,1)}, bf16[960,128]{1,0:T(8,128)(2,1)S(1)}, bf16[960,128]{1,0:T(8,128)(2,1)S(1)}, bf16[1920,128]{1,0:T(8,128)(2,1)...) custom-call(bf16[128,768]{1,0:T(8,128)(2,1)S(1)} %get-tuple-element., ...), custom_call_target="tpu_custom_call" | custom-call | flops 1 | bytes 1 | tf_op jit(solution)/shard_map/pallas_call | solution.py:722
  32.7 2.2 %shard_map.318 = (bf16[3552,128]{1,0:T(8,128)(2,1)S(1)}, bf16[3456,128]{1,0:T(8,128)(2,1)S(1)}, f32[128,768]{1,0:T(8,128)S(1)}, bf16[192,128]{1,0:T(8,128)(2,1)S...) custom-call(bf16[128,768]{1,0:T(8,128)(2,1)S(1)} %get-tuple-element.102.outer_low_ref,, ...), custom_call_target="tpu_custom_call" | custom-call | flops 1 | bytes 1 | tf_op jit(solution)/shard_map/pallas_call | solution.py:722
  34.9 1.6 %collective-permute-start.12 = (bf16[3456,128]{1,0:T(8,128)(2,1)S(1)}, bf16[3456,128]{1,0:T(8,128)(2,1)S(1)}, u32[]{:S(2)}, u32[]{:S(2)}) collective-permute-start(bf16[3456,128]{1,0:T(8,128)(2,1)S(1)} %get-tuple-element.133.own.sent), channel_id=1, source_target_pairs={{0,16},{4,20},{8,24},{12,28},{16,0},{20,4},{24,8},{28,12},{1,17},{... | collective-permute-start | bytes 2654216 | tf_op jit(solution)/shard_map/ppermute | solution.py:742
  36.5 1.5 %collective-permute-start.9 = (bf16[3552,128]{1,0:T(8,128)(2,1)S(1)}, bf16[3552,128]{1,0:T(8,128)(2,1)S(1)}, u32[]{:S(2)}, u32[]{:S(2)}) collective-permute-start(bf16[3552,128]{1,0:T(8,128)(2,1)S(1)} %get-tuple-element.127.own.sent), channel_id=1, source_target_pairs={{0,8},{4,12},{8,0},{12,4},{16,24},{20,28},{24,16},{28,20},{1,9},{5... | collective-permute-start | bytes 2727944 | tf_op jit(solution)/shard_map/ppermute | solution.py:742
  38.0 2.5 %collective-permute-start.3 = (bf16[192,128]{1,0:T(8,128)(2,1)S(1)}, bf16[192,128]{1,0:T(8,128)(2,1)S(1)}, u32[]{:S(2)}, u32[]{:S(2)}) collective-permute-start(bf16[192,128]{1,0:T(8,128)(2,1)S(1)} %get-tuple-element.118), channel_id=1, source_target_pairs={{0,1},{1,2},{2,3},{3,0},{4,5},{5,6},{6,7},{7,4},{8,9},{9,10},{10,1... | collective-permute-start | bytes 147464 | tf_op jit(solution)/shard_map/ppermute | solution.py:737
  40.5 0.9 collective-permute-start.4
  41.4 1.9 %collective-permute-start.5 = (bf16[192,128]{1,0:T(8,128)(2,1)S(1)}, bf16[192,128]{1,0:T(8,128)(2,1)S(1)}, u32[]{:S(2)}, u32[]{:S(2)}) collective-permute-start(bf16[192,128]{1,0:T(8,128)(2,1)S(1)} %get-tuple-element.120), channel_id=1, source_target_pairs={{0,3},{1,0},{2,1},{3,2},{4,7},{5,4},{6,5},{7,6},{8,11},{9,8},{10,9... | collective-permute-start | bytes 147464 | tf_op jit(solution)/shard_map/ppermute | solution.py:737
  43.4 5.3 %shard_map.319 = (bf16[3,512,512]{2,1,0:T(8,128)(2,1)S(1)}, bf16[192,512]{1,0:T(8,128)(2,1)S(1)}, bf16[192,512]{1,0:T(8,128)(2,1)S(1)}, bf16[192,512]{1,0:T(8,128)(2,1)S(1)}, f32[512,192]{1,0:T(8,128)S(1)}) custom-call(bf16[128,768]{1,0:T(8,128)(2,1)S(1)} %get-tuple-element.91.x0.x_ref, bf16[128,768]{1,0:T(8,128)(2,1)S(1)} %collective-permute-done.x1, ...), custom_call_target="tpu_custom_call" | custom-call | flops 1 | bytes 1 | tf_op jit(solution)/shard_map/pallas_call | solution.py:722
  48.7 2.1 %shard_map.320 = (bf16[576,128]{1,0:T(8,128)(2,1)S(1)}, bf16[576,128]{1,0:T(8,128)(2,1)S(1)}, bf16[576,128]{1,0:T(8,128)(2,1)S(1)}, bf16[576,128]{1,0:T(8,128)(2,1)S(1)}, f32[8,576]{1,0:T(8,128)S(1)}) custom-call(bf16[3,512,512]{2,1,0:T(8,128)(2,1)S(1)} %get-tuple-element.112.probs_ref, bf16[192,512]{1,0:T(8,128)(2,1)S(1)} %get-tuple-element.113.q_t_ref, ...), custom_call_target="tpu_custom_call" | custom-call | flops 1 | bytes 1 | tf_op jit(solution)/shard_map/pallas_call | solution.py:722
  50.8 1.6 %collective-permute-start.6 = (bf16[576,128]{1,0:T(8,128)(2,1)S(1)}, bf16[576,128]{1,0:T(8,128)(2,1)S(1)}, u32[]{:S(2)}, u32[]{:S(2)}) collective-permute-start(bf16[576,128]{1,0:T(8,128)(2,1)S(1)} %get-tuple-element.122.e1), channel_id=1, source_target_pairs={{0,3},{1,0},{2,1},{3,2},{4,7},{5,4},{6,5},{7,6},{8,11},{9,8},{10,9... | collective-permute-start | bytes 442376 | tf_op jit(solution)/shard_map/ppermute | solution.py:737
  52.4 3.6 %collective-permute-done.6.e1.after_and_out_0_ = bf16[576,128]{1,0:T(8,128)(2,1)S(1)} collective-permute-done((bf16[576,128]{1,0:T(8,128)(2,1)S(1)}, bf16[576,128]{1,0:T(8,128)(2,1)S(1)}, u32[]{:S(2)}, u32[]{:S(2)}) %collective-permute-start.6) | collective-permute-done | bytes 147488 | tf_op jit(solution)/shard_map/ppermute | solution.py:737
  56.2 1.2 %collective-permute-done.9.got.received = bf16[3552,128]{1,0:T(8,128)(2,1)S(1)} collective-permute-done((bf16[3552,128]{1,0:T(8,128)(2,1)S(1)}, bf16[3552,128]{1,0:T(8,128)(2,1)S(1)}, u32[]{:S(2)}, u32[]{:S(2)}) %collective-permute-start.9) | collective-permute-done | bytes 909344 | tf_op jit(solution)/shard_map/ppermute | solution.py:742
  57.5 2.2 %collective-permute-done.13.packed = bf16[6528,128]{1,0:T(8,128)(2,1)S(1)} collective-permute-done((bf16[6528,128]{1,0:T(8,128)(2,1)S(1)}, bf16[6528,128]{1,0:T(8,128)(2,1)S(1)}, u32[]{:S(2)}, u32[]{:S(2)}) %collective-permute-start.13) | collective-permute-done | bytes 1671200 | tf_op jit(solution)/shard_map/ppermute | solution.py:742
  59.7 1.2 %shard_map.326 = (bf16[96,3072]{1,0:T(8,128)(2,1)S(1)}, bf16[96,3072]{1,0:T(8,128)(2,1)S(1)}) custom-call(bf16[192,128]{1,0:T(8,128)(2,1)S(1)} %get-tuple-element.132.inner_own, bf16[3456,128]{1,0:T(8,128)(2,1)S(1)} %get-tuple-element.133.own.sent, bf16[3456,128]{1,0:T(8,128)(2,1)S(1)} %collective-permute-done.12.got.received, ...), custom_call_target="tpu_custom_call" | custom-call | flops 1 | bytes 1 | tf_op jit(solution)/shard_map/pallas_call | solution.py:722
  60.9 1.1 collective-permute-start.14
  62.0 1.0 shard_map.323
  63.0 1.6 %collective-permute-start.16 = (bf16[496,768]{1,0:T(8,128)(2,1)S(1)}, bf16[496,768]{1,0:T(8,128)(2,1)S(1)}, u32[]{:S(2)}, u32[]{:S(2)}) collective-permute-start(bf16[496,768]{1,0:T(8,128)(2,1)S(1)} %get-tuple-element.129.order_after), channel_id=1, source_target_pairs={{0,16},{4,20},{8,24},{12,28},{16,0},{20,4},{24,8},{28,12},{1,17},{... | collective-permute-start | bytes 2285576 | tf_op jit(solution)/shard_map/ppermute | solution.py:742
  64.6 0.9 shard_map.324
  65.6 2.7 %collective-permute-start.7 = (bf16[576,128]{1,0:T(8,128)(2,1)S(1)}, bf16[576,128]{1,0:T(8,128)(2,1)S(1)}, u32[]{:S(2)}, u32[]{:S(2)}) collective-permute-start(bf16[576,128]{1,0:T(8,128)(2,1)S(1)} %get-tuple-element.123.e2), channel_id=1, source_target_pairs={{0,2},{1,3},{2,0},{3,1},{4,6},{5,7},{6,4},{7,5},{8,10},{9,11},{10,... | collective-permute-start | bytes 442376 | tf_op jit(solution)/shard_map/ppermute | solution.py:737
  68.3 1.0 collective-permute-start.8
  69.4 9.7 %collective-permute-done.7.e2.rest_2_ = bf16[576,128]{1,0:T(8,128)(2,1)S(1)} collective-permute-done((bf16[576,128]{1,0:T(8,128)(2,1)S(1)}, bf16[576,128]{1,0:T(8,128)(2,1)S(1)}, u32[]{:S(2)}, u32[]{:S(2)}) %collective-permute-start.7) | collective-permute-done | bytes 147488 | tf_op jit(solution)/shard_map/ppermute | solution.py:737
  79.3 0.7 collective-permute-start.15
  80.3 2.3 %collective-permute-start.18 = (bf16[96,768]{1,0:T(8,128)(2,1)S(1)}, bf16[96,768]{1,0:T(8,128)(2,1)S(1)}, u32[]{:S(2)}, u32[]{:S(2)}) collective-permute-start(bf16[96,768]{1,0:T(8,128)(2,1)S(1)} %get-tuple-element.141), channel_id=1, source_target_pairs={{0,2},{1,3},{2,0},{3,1},{4,6},{5,7},{6,4},{7,5},{8,10},{9,11},{10,... | collective-permute-start | bytes 442376 | tf_op jit(solution)/shard_map/ppermute | solution.py:737
  82.6 4.7 %collective-permute-done.15.rest_0_ = bf16[208,576]{1,0:T(8,128)(2,1)S(1)} collective-permute-done((bf16[208,576]{1,0:T(8,128)(2,1)S(1)}, bf16[208,576]{1,0:T(8,128)(2,1)S(1)}, u32[]{:S(2)}, u32[]{:S(2)}) %collective-permute-start.15) | collective-permute-done | bytes 239648 | tf_op jit(solution)/shard_map/ppermute | solution.py:742
  88.2 3.5 %collective-permute-start.23 = (bf16[96,768]{1,0:T(8,128)(2,1)S(1)}, bf16[96,768]{1,0:T(8,128)(2,1)S(1)}, u32[]{:S(2)}, u32[]{:S(2)}) collective-permute-start(bf16[96,768]{1,0:T(8,128)(2,1)S(1)} %get-tuple-element.159), channel_id=1, source_target_pairs={{0,3},{1,0},{2,1},{3,2},{4,7},{5,4},{6,5},{7,6},{8,11},{9,8},{10,9... | collective-permute-start | bytes 442376 | tf_op jit(solution)/shard_map/ppermute | solution.py:737
  91.8 0.8 collective-permute-done.17.got
  92.5 0.8 shard_map.330
  94.2 2.0 %collective-permute-start.20 = (bf16[272,384]{1,0:T(8,128)(2,1)S(1)}, bf16[272,384]{1,0:T(8,128)(2,1)S(1)}, u32[]{:S(2)}, u32[]{:S(2)}) collective-permute-start(bf16[272,384]{1,0:T(8,128)(2,1)S(1)} %get-tuple-element.147), channel_id=1, source_target_pairs={{0,2},{1,3},{2,0},{3,1},{4,6},{5,7},{6,4},{7,5},{8,10},{9,11},{10,... | collective-permute-start | bytes 626696 | tf_op jit(solution)/shard_map/ppermute | solution.py:737
  96.2 2.8 %collective-permute-start.21 = (bf16[272,384]{1,0:T(8,128)(2,1)S(1)}, bf16[272,384]{1,0:T(8,128)(2,1)S(1)}, u32[]{:S(2)}, u32[]{:S(2)}) collective-permute-start(bf16[272,384]{1,0:T(8,128)(2,1)S(1)} %get-tuple-element.148), channel_id=1, source_target_pairs={{0,3},{1,0},{2,1},{3,2},{4,7},{5,4},{6,5},{7,6},{8,11},{9,8},{10,9... | collective-permute-start | bytes 626696 | tf_op jit(solution)/shard_map/ppermute | solution.py:737
  99.1 3.3 %shard_map.321 = bf16[128,768]{1,0:T(8,128)(2,1)} custom-call(bf16[576,128]{1,0:T(8,128)(2,1)S(1)} %get-tuple-element.121.e0, bf16[576,128]{1,0:T(8,128)(2,1)S(1)} %collective-permute-done.6.e1.after_and_out_0_, bf16[576,128]{1,0:T(8,128)(2,1)S(1)} %collective-permute-done.7.e2.rest_2_, bf16[576,128]{1,0:T(8,128)(2,1)S(1)} %collective-permute-done.8.e3.rest_3_, ...), custom_call_target="tpu_custom_call" | custom-call | flops 4000000000 | bytes 1 | tf_op jit(solution)/shard_map/pallas_call | solution.py:722
  102.4 0.8 shard_map.333
  103.8 8.0 %collective-permute-done.20.r2 = bf16[272,384]{1,0:T(8,128)(2,1)S(1)} collective-permute-done((bf16[272,384]{1,0:T(8,128)(2,1)S(1)}, bf16[272,384]{1,0:T(8,128)(2,1)S(1)}, u32[]{:S(2)}, u32[]{:S(2)}) %collective-permute-start.20) | collective-permute-done | bytes 208928 | tf_op jit(solution)/shard_map/ppermute | solution.py:737
  111.8 0.8 shard_map.332
  112.6 0.9 copy.36
  (54 shorter events, 4.7 us)
Async XLA Ops:
  0.7 22.4 %collective-permute-start.2 = (bf16[128,768]{1,0:T(8,128)(2,1)}, bf16[128,768]{1,0:T(8,128)(2,1)S(1)}, u32[]{:S(2)}, u32[]{:S(2)}) collective-permute-start(bf16[128,768]{1,0:T(8,128)(2,1)} %bitcast.5), channel_id=1, source_target_pairs={{0,3},{1,0},{2,1},{3,2},{4,7},{5,4},{6,5},{7,6},{8,11},{9,8},{10,9... | collective-permute-start | bytes 589832 | tf_op jit(solution)/shard_map/ppermute | solution.py:737
  5.8 17.3 %collective-permute-start.1 = (bf16[128,768]{1,0:T(8,128)(2,1)}, bf16[128,768]{1,0:T(8,128)(2,1)S(1)}, u32[]{:S(2)}, u32[]{:S(2)}) collective-permute-start(bf16[128,768]{1,0:T(8,128)(2,1)} %bitcast.6), channel_id=1, source_target_pairs={{0,2},{1,3},{2,0},{3,1},{4,6},{5,7},{6,4},{7,5},{8,10},{9,11},{10,... | collective-permute-start | bytes 589832 | tf_op jit(solution)/shard_map/ppermute | solution.py:737
  5.8 17.3 %collective-permute-start = (bf16[128,768]{1,0:T(8,128)(2,1)}, bf16[128,768]{1,0:T(8,128)(2,1)S(1)}, u32[]{:S(2)}, u32[]{:S(2)}) collective-permute-start(bf16[128,768]{1,0:T(8,128)(2,1)} %bitcast.7), channel_id=1, source_target_pairs={{0,1},{1,2},{2,3},{3,0},{4,5},{5,6},{6,7},{7,4},{8,9},{9,10},{10,1... | collective-permute-start | bytes 589832 | tf_op jit(solution)/shard_map/ppermute | solution.py:737
  7.7 2.3 %copy-start.1 = (bf16[3072,768]{1,0:T(8,128)(2,1)S(1)}, bf16[3072,768]{1,0:T(8,128)(2,1)}, u32[]{:S(2)}) copy-start(bf16[3072,768]{1,0:T(8,128)(2,1)} %w_outer.1) | copy-start | bytes 14155780
  10.0 1.3 %copy-start.2 = (bf16[768,768]{1,0:T(8,128)(2,1)S(1)}, bf16[768,768]{1,0:T(8,128)(2,1)}, u32[]{:S(2)}) copy-start(bf16[768,768]{1,0:T(8,128)(2,1)} %w_query.3) | copy-start | bytes 3538948
  11.3 1.3 %copy-start.4 = (bf16[768,768]{1,0:T(8,128)(2,1)S(1)}, bf16[768,768]{1,0:T(8,128)(2,1)}, u32[]{:S(2)}) copy-start(bf16[768,768]{1,0:T(8,128)(2,1)} %w_key.3) | copy-start | bytes 3538948
  12.6 1.3 %copy-start.6 = (bf16[768,768]{1,0:T(8,128)(2,1)S(1)}, bf16[768,768]{1,0:T(8,128)(2,1)}, u32[]{:S(2)}) copy-start(bf16[768,768]{1,0:T(8,128)(2,1)} %w_value.3) | copy-start | bytes 3538948
  13.9 0.9 copy-start.8
  14.8 0.9 copy-start.9
  15.7 0.7 copy-start.10
  16.4 0.7 copy-start.11
  17.1 0.7 copy-start.12
  17.7 2.3 %copy-start.13 = (bf16[768,3072]{1,0:T(8,128)(2,1)S(1)}, bf16[768,3072]{1,0:T(8,128)(2,1)}, u32[]{:S(2)}) copy-start(bf16[768,3072]{1,0:T(8,128)(2,1)} %w_inner.1) | copy-start | bytes 14155780
  23.1 6.1 %copy-start = (bf16[768,768]{1,0:T(8,128)(2,1)S(1)}, bf16[768,768]{1,0:T(8,128)(2,1)}, u32[]{:S(2)}) copy-start(bf16[768,768]{1,0:T(8,128)(2,1)} %w_output.3) | copy-start | bytes 3538948
  34.9 21.0 %collective-permute-start.12 = (bf16[3456,128]{1,0:T(8,128)(2,1)S(1)}, bf16[3456,128]{1,0:T(8,128)(2,1)S(1)}, u32[]{:S(2)}, u32[]{:S(2)}) collective-permute-start(bf16[3456,128]{1,0:T(8,128)(2,1)S(1)} %get-tuple-element.133.own.sent), channel_id=1, source_target_pairs={{0,16},{4,20},{8,24},{12,28},{16,0},{20,4},{24,8},{28,12},{1,17},{... | collective-permute-start | bytes 2654216 | tf_op jit(solution)/shard_map/ppermute | solution.py:742
  36.5 20.8 %collective-permute-start.9 = (bf16[3552,128]{1,0:T(8,128)(2,1)S(1)}, bf16[3552,128]{1,0:T(8,128)(2,1)S(1)}, u32[]{:S(2)}, u32[]{:S(2)}) collective-permute-start(bf16[3552,128]{1,0:T(8,128)(2,1)S(1)} %get-tuple-element.127.own.sent), channel_id=1, source_target_pairs={{0,8},{4,12},{8,0},{12,4},{16,24},{20,28},{24,16},{28,20},{1,9},{5... | collective-permute-start | bytes 2727944 | tf_op jit(solution)/shard_map/ppermute | solution.py:742
  38.0 10.6 %collective-permute-start.3 = (bf16[192,128]{1,0:T(8,128)(2,1)S(1)}, bf16[192,128]{1,0:T(8,128)(2,1)S(1)}, u32[]{:S(2)}, u32[]{:S(2)}) collective-permute-start(bf16[192,128]{1,0:T(8,128)(2,1)S(1)} %get-tuple-element.118), channel_id=1, source_target_pairs={{0,1},{1,2},{2,3},{3,0},{4,5},{5,6},{6,7},{7,4},{8,9},{9,10},{10,1... | collective-permute-start | bytes 147464 | tf_op jit(solution)/shard_map/ppermute | solution.py:737
  40.5 8.2 %collective-permute-start.4 = (bf16[192,128]{1,0:T(8,128)(2,1)S(1)}, bf16[192,128]{1,0:T(8,128)(2,1)S(1)}, u32[]{:S(2)}, u32[]{:S(2)}) collective-permute-start(bf16[192,128]{1,0:T(8,128)(2,1)S(1)} %get-tuple-element.119), channel_id=1, source_target_pairs={{0,2},{1,3},{2,0},{3,1},{4,6},{5,7},{6,4},{7,5},{8,10},{9,11},{10,... | collective-permute-start | bytes 147464 | tf_op jit(solution)/shard_map/ppermute | solution.py:737
  41.4 7.3 %collective-permute-start.5 = (bf16[192,128]{1,0:T(8,128)(2,1)S(1)}, bf16[192,128]{1,0:T(8,128)(2,1)S(1)}, u32[]{:S(2)}, u32[]{:S(2)}) collective-permute-start(bf16[192,128]{1,0:T(8,128)(2,1)S(1)} %get-tuple-element.120), channel_id=1, source_target_pairs={{0,3},{1,0},{2,1},{3,2},{4,7},{5,4},{6,5},{7,6},{8,11},{9,8},{10,9... | collective-permute-start | bytes 147464 | tf_op jit(solution)/shard_map/ppermute | solution.py:737
  50.8 5.2 %collective-permute-start.6 = (bf16[576,128]{1,0:T(8,128)(2,1)S(1)}, bf16[576,128]{1,0:T(8,128)(2,1)S(1)}, u32[]{:S(2)}, u32[]{:S(2)}) collective-permute-start(bf16[576,128]{1,0:T(8,128)(2,1)S(1)} %get-tuple-element.122.e1), channel_id=1, source_target_pairs={{0,3},{1,0},{2,1},{3,2},{4,7},{5,4},{6,5},{7,6},{8,11},{9,8},{10,9... | collective-permute-start | bytes 442376 | tf_op jit(solution)/shard_map/ppermute | solution.py:737
  56.1 3.6 %collective-permute-start.13 = (bf16[6528,128]{1,0:T(8,128)(2,1)S(1)}, bf16[6528,128]{1,0:T(8,128)(2,1)S(1)}, u32[]{:S(2)}, u32[]{:S(2)}) collective-permute-start(bf16[6528,128]{1,0:T(8,128)(2,1)S(1)} %shard_map.325), channel_id=1, source_target_pairs={{0,4},{4,0},{8,12},{12,8},{16,20},{20,16},{24,28},{28,24},{1,5},{5... | collective-permute-start | bytes 5013512 | tf_op jit(solution)/shard_map/ppermute | solution.py:742
  57.4 4.6 %collective-permute-start.10 = (bf16[5184,128]{1,0:T(8,128)(2,1)S(1)}, bf16[5184,128]{1,0:T(8,128)(2,1)S(1)}, u32[]{:S(2)}, u32[]{:S(2)}) collective-permute-start(bf16[5184,128]{1,0:T(8,128)(2,1)S(1)} %shard_map.322), channel_id=1, source_target_pairs={{0,4},{4,0},{8,12},{12,8},{16,20},{20,16},{24,28},{28,24},{1,5},{5... | collective-permute-start | bytes 3981320 | tf_op jit(solution)/shard_map/ppermute | solution.py:742
  60.9 18.2 %collective-permute-start.14 = (bf16[96,3072]{1,0:T(8,128)(2,1)S(1)}, bf16[96,3072]{1,0:T(8,128)(2,1)S(1)}, u32[]{:S(2)}, u32[]{:S(2)}) collective-permute-start(bf16[96,3072]{1,0:T(8,128)(2,1)S(1)} %get-tuple-element.135), channel_id=1, source_target_pairs={{0,8},{4,12},{8,0},{12,4},{16,24},{20,28},{24,16},{28,20},{1,9},{5... | collective-permute-start | bytes 1769480 | tf_op jit(solution)/shard_map/ppermute | solution.py:742
  63.0 19.5 %collective-permute-start.16 = (bf16[496,768]{1,0:T(8,128)(2,1)S(1)}, bf16[496,768]{1,0:T(8,128)(2,1)S(1)}, u32[]{:S(2)}, u32[]{:S(2)}) collective-permute-start(bf16[496,768]{1,0:T(8,128)(2,1)S(1)} %get-tuple-element.129.order_after), channel_id=1, source_target_pairs={{0,16},{4,20},{8,24},{12,28},{16,0},{20,4},{24,8},{28,12},{1,17},{... | collective-permute-start | bytes 2285576 | tf_op jit(solution)/shard_map/ppermute | solution.py:742
  65.5 13.6 %collective-permute-start.11 = (bf16[400,576]{1,0:T(8,128)(2,1)S(1)}, bf16[400,576]{1,0:T(8,128)(2,1)S(1)}, u32[]{:S(2)}, u32[]{:S(2)}) collective-permute-start(bf16[400,576]{1,0:T(8,128)(2,1)S(1)} %get-tuple-element.131), channel_id=1, source_target_pairs={{0,4},{4,0},{8,12},{12,8},{16,20},{20,16},{24,28},{28,24},{1,5},{5... | collective-permute-start | bytes 1382408 | tf_op jit(solution)/shard_map/ppermute | solution.py:742
  65.6 13.5 %collective-permute-start.7 = (bf16[576,128]{1,0:T(8,128)(2,1)S(1)}, bf16[576,128]{1,0:T(8,128)(2,1)S(1)}, u32[]{:S(2)}, u32[]{:S(2)}) collective-permute-start(bf16[576,128]{1,0:T(8,128)(2,1)S(1)} %get-tuple-element.123.e2), channel_id=1, source_target_pairs={{0,2},{1,3},{2,0},{3,1},{4,6},{5,7},{6,4},{7,5},{8,10},{9,11},{10,... | collective-permute-start | bytes 442376 | tf_op jit(solution)/shard_map/ppermute | solution.py:737
  68.3 10.8 %collective-permute-start.8 = (bf16[576,128]{1,0:T(8,128)(2,1)S(1)}, bf16[576,128]{1,0:T(8,128)(2,1)S(1)}, u32[]{:S(2)}, u32[]{:S(2)}) collective-permute-start(bf16[576,128]{1,0:T(8,128)(2,1)S(1)} %get-tuple-element.124.e3), channel_id=1, source_target_pairs={{0,1},{1,2},{2,3},{3,0},{4,5},{5,6},{6,7},{7,4},{8,9},{9,10},{10,1... | collective-permute-start | bytes 442376 | tf_op jit(solution)/shard_map/ppermute | solution.py:737
  79.3 8.0 %collective-permute-start.15 = (bf16[208,576]{1,0:T(8,128)(2,1)S(1)}, bf16[208,576]{1,0:T(8,128)(2,1)S(1)}, u32[]{:S(2)}, u32[]{:S(2)}) collective-permute-start(bf16[208,576]{1,0:T(8,128)(2,1)S(1)} %get-tuple-element.137), channel_id=1, source_target_pairs={{0,8},{4,12},{8,0},{12,4},{16,24},{20,28},{24,16},{28,20},{1,9},{5... | collective-permute-start | bytes 718856 | tf_op jit(solution)/shard_map/ppermute | solution.py:742
  80.0 19.1 %copy-start.7 = (bf16[768,768]{1,0:T(8,128)(2,1)S(1)}, bf16[768,768]{1,0:T(8,128)(2,1)}, u32[]{:S(2)}) copy-start(bf16[768,768]{1,0:T(8,128)(2,1)} %w_value.3) | copy-start | bytes 3538948
  80.3 11.5 %collective-permute-start.18 = (bf16[96,768]{1,0:T(8,128)(2,1)S(1)}, bf16[96,768]{1,0:T(8,128)(2,1)S(1)}, u32[]{:S(2)}, u32[]{:S(2)}) collective-permute-start(bf16[96,768]{1,0:T(8,128)(2,1)S(1)} %get-tuple-element.141), channel_id=1, source_target_pairs={{0,2},{1,3},{2,0},{3,1},{4,6},{5,7},{6,4},{7,5},{8,10},{9,11},{10,... | collective-permute-start | bytes 442376 | tf_op jit(solution)/shard_map/ppermute | solution.py:737
  87.3 11.8 %copy-start.3 = (bf16[768,768]{1,0:T(8,128)(2,1)S(1)}, bf16[768,768]{1,0:T(8,128)(2,1)}, u32[]{:S(2)}) copy-start(bf16[768,768]{1,0:T(8,128)(2,1)} %w_query.3) | copy-start | bytes 3538948
  87.3 11.8 %copy-start.5 = (bf16[768,768]{1,0:T(8,128)(2,1)S(1)}, bf16[768,768]{1,0:T(8,128)(2,1)}, u32[]{:S(2)}) copy-start(bf16[768,768]{1,0:T(8,128)(2,1)} %w_key.3) | copy-start | bytes 3538948
  87.4 5.2 %collective-permute-start.17 = (bf16[112,576]{1,0:T(8,128)(2,1)S(1)}, bf16[112,576]{1,0:T(8,128)(2,1)S(1)}, u32[]{:S(2)}, u32[]{:S(2)}) collective-permute-start(bf16[112,576]{1,0:T(8,128)(2,1)S(1)} %get-tuple-element.139), channel_id=1, source_target_pairs={{0,16},{4,20},{8,24},{12,28},{16,0},{20,4},{24,8},{28,12},{1,17},{... | collective-permute-start | bytes 387080 | tf_op jit(solution)/shard_map/ppermute | solution.py:742
  87.9 14.4 %collective-permute-start.22 = (bf16[96,768]{1,0:T(8,128)(2,1)S(1)}, bf16[96,768]{1,0:T(8,128)(2,1)S(1)}, u32[]{:S(2)}, u32[]{:S(2)}) collective-permute-start(bf16[96,768]{1,0:T(8,128)(2,1)S(1)} %get-tuple-element.158), channel_id=1, source_target_pairs={{0,1},{1,2},{2,3},{3,0},{4,5},{5,6},{6,7},{7,4},{8,9},{9,10},{10,1... | collective-permute-start | bytes 442376 | tf_op jit(solution)/shard_map/ppermute | solution.py:737
  88.2 14.1 %collective-permute-start.23 = (bf16[96,768]{1,0:T(8,128)(2,1)S(1)}, bf16[96,768]{1,0:T(8,128)(2,1)S(1)}, u32[]{:S(2)}, u32[]{:S(2)}) collective-permute-start(bf16[96,768]{1,0:T(8,128)(2,1)S(1)} %get-tuple-element.159), channel_id=1, source_target_pairs={{0,3},{1,0},{2,1},{3,2},{4,7},{5,4},{6,5},{7,6},{8,11},{9,8},{10,9... | collective-permute-start | bytes 442376 | tf_op jit(solution)/shard_map/ppermute | solution.py:737
  93.9 10.0 %collective-permute-start.19 = (bf16[272,384]{1,0:T(8,128)(2,1)S(1)}, bf16[272,384]{1,0:T(8,128)(2,1)S(1)}, u32[]{:S(2)}, u32[]{:S(2)}) collective-permute-start(bf16[272,384]{1,0:T(8,128)(2,1)S(1)} %get-tuple-element.146), channel_id=1, source_target_pairs={{0,1},{1,2},{2,3},{3,0},{4,5},{5,6},{6,7},{7,4},{8,9},{9,10},{10,1... | collective-permute-start | bytes 626696 | tf_op jit(solution)/shard_map/ppermute | solution.py:737
  94.2 17.6 %collective-permute-start.20 = (bf16[272,384]{1,0:T(8,128)(2,1)S(1)}, bf16[272,384]{1,0:T(8,128)(2,1)S(1)}, u32[]{:S(2)}, u32[]{:S(2)}) collective-permute-start(bf16[272,384]{1,0:T(8,128)(2,1)S(1)} %get-tuple-element.147), channel_id=1, source_target_pairs={{0,2},{1,3},{2,0},{3,1},{4,6},{5,7},{6,4},{7,5},{8,10},{9,11},{10,... | collective-permute-start | bytes 626696 | tf_op jit(solution)/shard_map/ppermute | solution.py:737
  96.2 15.6 %collective-permute-start.21 = (bf16[272,384]{1,0:T(8,128)(2,1)S(1)}, bf16[272,384]{1,0:T(8,128)(2,1)S(1)}, u32[]{:S(2)}, u32[]{:S(2)}) collective-permute-start(bf16[272,384]{1,0:T(8,128)(2,1)S(1)} %get-tuple-element.148), channel_id=1, source_target_pairs={{0,3},{1,0},{2,1},{3,2},{4,7},{5,4},{6,5},{7,6},{8,11},{9,8},{10,9... | collective-permute-start | bytes 626696 | tf_op jit(solution)/shard_map/ppermute | solution.py:737
